TPU v7x, 128 devices: a whole 4x4x4 slice. The times are simulated.
128 devices in a mesh: img: 8 (over y, core), pair: 16 (over z, x).
Axes of the slice: x: 4, y: 4, z: 4, core: 2. Of those that a mesh axis runs over, the one named last changes fastest.
Arguments:
- encoder_tokens: bfloat16 [4096, 16, 1024], P(('img', 'pair')), may hold values from -6 to 6
- pair_owner: int32 [4096, 2], P(('img', 'pair')), may hold values from 0 to 127, as said below
- pair_local: int32 [4096, 2], P(('img', 'pair')), may hold values from 0 to 31
- w_embed: bfloat16 [1024, 768], replicated, may hold values from -0.1875 to 0.1875
- gain_query: float32 [768], replicated, may hold values from 0.5 to 14
- gain_key: float32 [768], replicated, may hold values from 0.5 to 14
- gain_out: float32 [768], replicated, may hold values from 0.25 to 1.75
- w_query: bfloat16 [768, 768], replicated, may hold values from -0.21875 to 0.21875
- w_key: bfloat16 [768, 768], replicated, may hold values from -0.21875 to 0.21875
- w_value: bfloat16 [768, 768], replicated, may hold values from -0.21875 to 0.21875
- w_out: bfloat16 [768, 768], replicated, may hold values from -0.21875 to 0.21875
- w_head: bfloat16 [768, 1024], replicated, may hold values from -0.21875 to 0.21875
Outputs:
- image_sums: bfloat16 [4096, 16, 1024], P(('img', 'pair'))
Inputs may be any that keep to these rules, and one draw needn't show every extreme that they name: `pair_owner`: within the 32 rows of one device, the 64 entries are all different; one block value appears in every device's rows.
All inputs are finite; a program needn't handle non-finite values.
Results may differ from a plain program's by a relative error of at most 0.02.
The roundings to bfloat16 on the way count: a program that leaves them out, or rounds other values in their place, can miss the bound.
Values may be sent and summed in bfloat16 or wider, within the bound.
No kernel may reach another device: no remote copies, remote signals or barrier semaphores. Data moves between devices by JAX's collectives and lax.ppermute only.
A program may use at most 128 MiB of HBM per device.

v0:
```python
import functools

import jax
import jax.numpy as jnp
from jax import lax
from jax.experimental import pallas as pl
from jax.experimental.pallas import tpu as pltpu
from jax.sharding import PartitionSpec as P

HEADS = 12
HD = 64
TOK = 16
AXES = ("img", "pair")
GROUP = 8
BF16 = jnp.bfloat16
F32 = jnp.float32
MIB = 1024 * 1024


def exchange(blocks):
    return lax.all_to_all(blocks, AXES, split_axis=0, concat_axis=0, tiled=True)


def dot(a, b, contract):
    return lax.dot_general(a, b, (contract, ((), ())), preferred_element_type=F32)


def normalised(values):
    mean = jnp.mean(values, axis=-1, keepdims=True)
    centred = values - mean
    spread = jnp.mean(centred * centred, axis=-1, keepdims=True)
    return centred * lax.rsqrt(spread + 1e-05)


def fetch_kernel(asked, table, out, sem):
    devices = out.shape[0]
    owned = table.shape[0]

    def send(d, carry):
        image = jnp.clip(asked[d], 0, owned - 1)
        pltpu.make_async_copy(table.at[image], out.at[d], sem).start()
        return carry

    lax.fori_loop(0, devices, send, 0, unroll=8)
    pltpu.make_async_copy(out, out, sem).wait()


def fetch(asked, table, devices):
    return pl.pallas_call(
        fetch_kernel,
        out_shape=jax.ShapeDtypeStruct((devices,) + table.shape[1:], table.dtype),
        in_specs=[
            pl.BlockSpec(memory_space=pltpu.SMEM),
            pl.BlockSpec(memory_space=pltpu.VMEM),
        ],
        out_specs=pl.BlockSpec(memory_space=pl.ANY),
        scratch_shapes=[pltpu.SemaphoreType.DMA],
        name="fetch",
    )(asked, table)


def decode_kernel(
    owners,
    incoming,
    gain_query,
    gain_key,
    gain_out,
    w_query,
    w_key,
    w_value_t,
    w_out,
    out,
    ends,
    result,
    attended_t,
    in_sem,
    out_sem,
):
    images = ends.shape[0]
    width = ends.shape[2]
    step = 16
    rows = step * TOK
    block = GROUP * TOK

    def bring(i, carry):
        pltpu.make_async_copy(incoming.at[owners[i]], ends.at[i], in_sem).start()
        return carry

    lax.fori_loop(0, images, bring, 0, unroll=8)
    pltpu.make_async_copy(ends, ends, in_sem).wait()

    lane_image = lax.broadcasted_iota(jnp.int32, (TOK, block), 1) // TOK
    row_image = lax.broadcasted_iota(jnp.int32, (block, block), 0) // TOK
    column_image = lax.broadcasted_iota(jnp.int32, (block, block), 1) // TOK
    partner = ((row_image ^ 1) == column_image).astype(F32).astype(BF16)
    lane_head = lax.broadcasted_iota(jnp.int32, (block, 2 * HD), 1) // HD
    head_mask = [(lane_head == h).astype(F32).astype(BF16) for h in range(2)]

    def one(it, carry):
        x = ends[pl.ds(it * step, step)].reshape(rows, width).astype(F32)
        xn = normalised(x)
        query_in = (xn * gain_query[...]).astype(BF16)
        context_in = (xn * gain_key[...]).astype(BF16)
        query = dot(query_in, w_query[...], ((1,), (0,))).astype(BF16)
        key = dot(context_in, w_key[...], ((1,), (0,))).astype(BF16)
        value_t = dot(w_value_t[...], context_in, ((1,), (1,))).astype(BF16)
        for g in range(rows // block):
            at = slice(g * block, (g + 1) * block)
            for pair in range(HEADS // 2):
                lanes = slice(pair * 2 * HD, (pair + 1) * 2 * HD)
                q = query[at, lanes]
                k = key[at, lanes]
                for h in range(2):
                    s_t = dot(k * head_mask[h], q, ((1,), (1,)))
                    parts = [s_t[j * TOK:(j + 1) * TOK] for j in range(GROUP)]
                    scores = parts[1]
                    for i in range(1, GROUP):
                        scores = jnp.where(lane_image == i, parts[i ^ 1], scores)
                    scores = scores * (HD ** -0.5)
                    top = jnp.max(scores, axis=0, keepdims=True)
                    e = jnp.exp(scores - top)
                    weights = (e / jnp.sum(e, axis=0, keepdims=True)).astype(BF16)
                    p_t = jnp.concatenate([weights] * GROUP, axis=0) * partner
                    head = 2 * pair + h
                    v_t = value_t[head * HD:(head + 1) * HD, at]
                    attended_t[head * HD:(head + 1) * HD, at] = dot(
                        v_t, p_t, ((1,), (0,))
                    ).astype(BF16)
        hidden = x + dot(attended_t[...], w_out[...], ((0,), (0,)))
        head_in = (normalised(hidden) * gain_out[...]).astype(BF16)
        result[pl.ds(it * step, step)] = head_in.reshape(step, TOK, width)

        def give(i, carry):
            i = it * step + i
            pltpu.make_async_copy(result.at[i], out.at[owners[i]], out_sem).start()
            return carry

        lax.fori_loop(0, step, give, 0, unroll=8)
        return carry

    lax.fori_loop(0, images // step, one, 0)
    pltpu.make_async_copy(result, result, out_sem).wait()


def decode(owners, incoming, gain_query, gain_key, gain_out, w_query, w_key, w_value_t, w_out):
    images = owners.shape[0]
    devices, tokens, width = incoming.shape
    vmem = pl.BlockSpec(memory_space=pltpu.VMEM)
    rows = 16 * tokens
    return pl.pallas_call(
        decode_kernel,
        out_shape=jax.ShapeDtypeStruct(incoming.shape, BF16),
        in_specs=[
            pl.BlockSpec(memory_space=pltpu.SMEM),
            pl.BlockSpec(memory_space=pl.ANY),
        ] + [vmem] * 7,
        out_specs=pl.BlockSpec(memory_space=pl.ANY),
        scratch_shapes=[
            pltpu.VMEM((images, tokens, width), BF16),
            pltpu.VMEM((images, tokens, width), BF16),
            pltpu.VMEM((width, rows), BF16),
            pltpu.SemaphoreType.DMA,
            pltpu.SemaphoreType.DMA,
        ],
        compiler_params=pltpu.CompilerParams(vmem_limit_bytes=40 * MIB),
        name="decode",
    )(owners, incoming, gain_query, gain_key, gain_out, w_query, w_key, w_value_t, w_out)


def total_kernel(asked, returned, w_head, out, arrived, sums, sem):
    devices, tokens, width = arrived.shape
    owned = out.shape[0]
    copy = pltpu.make_async_copy(returned, arrived, sem)
    copy.start()
    sums[...] = jnp.zeros_like(sums)
    copy.wait()

    def add(d, carry):
        image = jnp.where(asked[d] >= 0, asked[d], owned)
        sums[image] += arrived[d].astype(F32)
        return carry

    lax.fori_loop(0, devices, add, 0, unroll=4)
    total = sums[:owned].reshape(owned * tokens, width)
    upper = total.astype(BF16)
    lower = (total - upper.astype(F32)).astype(BF16)
    head = dot(upper, w_head[...], ((1,), (0,))) + dot(lower, w_head[...], ((1,), (0,)))
    out[...] = head.astype(BF16).reshape(out.shape)


def total(asked, returned, w_head, owned):
    devices, tokens, width = returned.shape
    return pl.pallas_call(
        total_kernel,
        out_shape=jax.ShapeDtypeStruct((owned, tokens, w_head.shape[1]), BF16),
        in_specs=[
            pl.BlockSpec(memory_space=pltpu.SMEM),
            pl.BlockSpec(memory_space=pl.ANY),
            pl.BlockSpec(memory_space=pltpu.VMEM),
        ],
        out_specs=pl.BlockSpec(memory_space=pltpu.VMEM),
        scratch_shapes=[
            pltpu.VMEM(returned.shape, BF16),
            pltpu.VMEM((owned + 1, tokens, width), F32),
            pltpu.SemaphoreType.DMA,
        ],
        compiler_params=pltpu.CompilerParams(vmem_limit_bytes=40 * MIB),
        name="total",
    )(asked, returned, w_head)


def on_device(
    encoder_tokens,
    pair_owner,
    pair_local,
    w_embed,
    gain_query,
    gain_key,
    gain_out,
    w_query,
    w_key,
    w_value,
    w_out,
    w_head,
):
    devices = lax.axis_size(AXES)
    owned, tokens, _ = encoder_tokens.shape
    owners = pair_owner.reshape(-1)
    local = pair_local.reshape(-1)
    matches = owners[:, None] == jnp.arange(devices, dtype=jnp.int32)[None, :]
    wanted = jnp.sum(jnp.where(matches, local[:, None] + 1, 0), axis=0) - 1
    asked = exchange(wanted[:, None])[:, 0]
    table = jnp.dot(
        encoder_tokens.reshape(owned * tokens, -1), w_embed, preferred_element_type=F32
    ).astype(BF16).reshape(owned, tokens, -1)
    incoming = exchange(fetch(asked, table, devices))
    going_back = decode(
        owners,
        incoming,
        gain_query[None],
        gain_key[None],
        gain_out[None],
        w_query,
        w_key,
        w_value.T,
        w_out,
    )
    return total(asked, exchange(going_back), w_head, owned)


def solution(mesh):
    spec = P(AXES)
    return jax.shard_map(
        on_device,
        mesh=mesh,
        in_specs=(spec,) * 3 + (P(),) * 9,
        out_specs=spec,
        check_vma=False,
    )
```

profile of v0, /device:TPU:1, one launch (start us, length us, event | category | flops | bytes accessed | tf_op | source)
XLA Modules:
  0.0 160.7 jit_solution(211590141909048734)
XLA Ops:
  0.0 0.0 copy-start
  0.0 0.9 copy.27
  0.9 0.1 eq.15.owners
  1.0 0.7 broadcast_add_fusion
  1.7 0.1 copy.28
  1.8 0.1 add.26
  1.9 0.1 select_reduce_fusion
  2.0 0.7 copy.29
  2.7 11.5 %all-to-all-start = ((s32[128,1,1]{2,1,0:T(1,128)}), s32[128,1,1]{2,1,0:T(1,128)S(1)}, u32[]{:S(2)}, u32[]{:S(2)}) async-start(s32[128,1,1]{2,1,0:T(1,128)} %copy.29), calls=%async_computation | async-start | bytes 131072 | tf_op jit(solution)/shard_map/all_to_all | solution.py:21
  14.2 0.0 copy-done
  14.2 3.1 %convolution_convert_fusion = bf16[512,768]{1,0:T(8,128)(2,1)} fusion(bf16[512,1024]{1,0:T(8,128)(2,1)} %bitcast.9, bf16[1024,768]{1,0:T(8,128)(2,1)S(1)} %copy-done), kind=kOutput, calls=%fused_computation | convolution fusion | flops 805699584 | bytes 3407872 | tf_op jit(solution)/shard_map/dot_general | solution.py:233
  17.3 6.7 %all-to-all-done = s32[128,1,1]{2,1,0:T(1,128)S(1)} async-done(((s32[128,1,1]{2,1,0:T(1,128)}), s32[128,1,1]{2,1,0:T(1,128)S(1)}, u32[]{:S(2)}, u32[]{:S(2)}) %all-to-all-start) | async-done | bytes 544 | tf_op jit(solution)/shard_map/all_to_all | solution.py:21
  24.0 2.8 %reduce.asked = s32[128]{0:T(128)} reduce(s32[128,1,1]{2,1,0:T(1,128)S(1)} %all-to-all-done, s32[]{:T(128)} %constant.2.clone.1), dimensions={1,2}, to_apply=%all_to_all.10.reduce_sub_computation | reduce | bytes 1028 | tf_op jit(solution)/shard_map/all_to_all | solution.py:21
  26.8 2.8 %fetch.1 = bf16[128,16,768]{2,1,0:T(8,128)(2,1)} custom-call(s32[128]{0:T(128)} %reduce.asked, bf16[32,16,768]{2,1,0:T(8,128)(2,1)} %bitcast.8), custom_call_target="tpu_custom_call" | custom-call | tf_op jit(solution)/shard_map/fetch/pallas_call | solution.py:49
  29.7 5.3 %all-to-all-start.1 = ((bf16[128,16,768]{2,1,0:T(8,128)(2,1)}), bf16[128,16,768]{2,1,0:T(8,128)(2,1)}, u32[]{:S(2)}, u32[]{:S(2)}) async-start(bf16[128,16,768]{2,1,0:T(8,128)(2,1)} %fetch.1), calls=%async_computation.1 | async-start | bytes 6291456 | tf_op jit(solution)/shard_map/all_to_all | solution.py:21
  34.9 0.0 copy-start.6
  35.0 0.0 copy-start.7
  35.0 0.0 copy-start.8
  35.0 1.6 copy.30
  36.6 0.0 copy-done.6
  36.6 0.0 copy-done.7
  36.6 0.0 copy-done.8
  36.6 38.7 %all-to-all-done.1.incoming = bf16[128,16,768]{2,1,0:T(8,128)(2,1)} async-done(((bf16[128,16,768]{2,1,0:T(8,128)(2,1)}), bf16[128,16,768]{2,1,0:T(8,128)(2,1)}, u32[]{:S(2)}, u32[]{:S(2)}) %all-to-all-start.1) | async-done | bytes 3145760 | tf_op jit(solution)/shard_map/all_to_all | solution.py:21
  75.3 1.3 copy-done.2
  76.6 1.3 copy-done.3
  77.9 1.3 copy-done.4
  79.1 31.6 %decode.1 = bf16[128,16,768]{2,1,0:T(8,128)(2,1)S(1)} custom-call(s32[64]{0:T(128)S(1)} %eq.15.owners, bf16[128,16,768]{2,1,0:T(8,128)(2,1)} %all-to-all-done.1.incoming, f32[1,768]{1,0:T(1,128)S(1)} %broadcast_in_dim.25.gain_query, f32[1,768]{1,0:T(1,128)S(1)} %broadcast_in_dim.26.gain_key, f32[1,768]{1,0:T(1,128)S(1)} %broadcast_in_dim.27.gain_out, ...), custom_call_target="tpu_custom_call" | custom-call | tf_op jit(solution)/shard_map/decode/pallas_call | solution.py:150
  110.8 0.0 copy-start.1
  110.8 0.0 copy-start.5
  110.8 45.2 %all_to_all.16.returned = bf16[128,16,768]{2,1,0:T(8,128)(2,1)S(1)} all-to-all(bf16[128,16,768]{2,1,0:T(8,128)(2,1)S(1)} %decode.1), channel_id=1, replica_groups=mesh['img'=8,'pair'=16] {'img','pair'}, dimensions={0} | all-to-all | bytes 6291456 | tf_op jit(solution)/shard_map/all_to_all | solution.py:21
  156.1 0.0 copy-done.5
  156.1 4.6 %total.1 = bf16[32,16,1024]{2,1,0:T(8,128)(2,1)} custom-call(s32[128]{0:T(128)S(1)} %copy-done.5, bf16[128,16,768]{2,1,0:T(8,128)(2,1)S(1)} %all_to_all.16.returned, bf16[768,1024]{1,0:T(8,128)(2,1)S(1)} %copy-done.1), custom_call_target="tpu_custom_call" | custom-call | tf_op jit(solution)/shard_map/total/pallas_call | solution.py:193
  (8 shorter events, 0.0 us)
Async XLA Ops:
  0.0 14.2 %copy-start = (bf16[1024,768]{1,0:T(8,128)(2,1)S(1)}, bf16[1024,768]{1,0:T(8,128)(2,1)}, u32[]{:S(2)}) copy-start(bf16[1024,768]{1,0:T(8,128)(2,1)} %param.15) | copy-start | bytes 4718596
  2.7 21.3 %all-to-all-start = ((s32[128,1,1]{2,1,0:T(1,128)}), s32[128,1,1]{2,1,0:T(1,128)S(1)}, u32[]{:S(2)}, u32[]{:S(2)}) async-start(s32[128,1,1]{2,1,0:T(1,128)} %copy.29), calls=%async_computation | async-start | bytes 131072 | tf_op jit(solution)/shard_map/all_to_all | solution.py:21
  29.7 45.7 %all-to-all-start.1 = ((bf16[128,16,768]{2,1,0:T(8,128)(2,1)}), bf16[128,16,768]{2,1,0:T(8,128)(2,1)}, u32[]{:S(2)}, u32[]{:S(2)}) async-start(bf16[128,16,768]{2,1,0:T(8,128)(2,1)} %fetch.1), calls=%async_computation.1 | async-start | bytes 6291456 | tf_op jit(solution)/shard_map/all_to_all | solution.py:21
  34.9 1.6 %copy-start.6 = (f32[768]{0:T(1024)S(1)}, f32[768]{0:T(1024)}, u32[]{:S(2)}) copy-start(f32[768]{0:T(1024)} %param.16) | copy-start | bytes 9220
  35.0 1.6 %copy-start.7 = (f32[768]{0:T(1024)S(1)}, f32[768]{0:T(1024)}, u32[]{:S(2)}) copy-start(f32[768]{0:T(1024)} %param.17) | copy-start | bytes 9220
  35.0 1.6 %copy-start.8 = (f32[768]{0:T(1024)S(1)}, f32[768]{0:T(1024)}, u32[]{:S(2)}) copy-start(f32[768]{0:T(1024)} %param.18) | copy-start | bytes 9220
  75.3 1.3 copy-start.2
  76.6 1.3 copy-start.3
  77.9 1.3 copy-start.4
  110.8 45.3 %copy-start.1 = (bf16[768,1024]{1,0:T(8,128)(2,1)S(1)}, bf16[768,1024]{1,0:T(8,128)(2,1)}, u32[]{:S(2)}) copy-start(bf16[768,1024]{1,0:T(8,128)(2,1)} %w_head.1) | copy-start | bytes 4718596
  110.8 45.2 %copy-start.5 = (s32[128]{0:T(128)S(1)}, s32[128]{0:T(128)}, u32[]{:S(2)}) copy-start(s32[128]{0:T(128)} %reduce.asked) | copy-start | bytes 1540
where the time goes:
time: 161 us
  waiting for transfers between devices  45.4 us (28%)
  blocking collectives  45.2 us (28%)
  Pallas kernels  39.1 us (24%)
  starting transfers between devices  16.8 us (10%)
  local copies, waits for them, and re-layouts  7.34 us (5%)
  other arithmetic  3.63 us (2%)
  matrix products  3.08 us (2%)
    all_to_all x2, waiting for transfers between devices, exchange(): return lax.all_to_all(blocks, AXES, split_axis=0, concat_axis=0, tiled=True)  45.4 us
    all_to_all x1, blocking collectives, exchange(): return lax.all_to_all(blocks, AXES, split_axis=0, concat_axis=0, tiled=True)  45.2 us
    pallas_call x1, Pallas kernels, decode(): pl.pallas_call(decode_kernel, out_shape=jax.ShapeDtypeStruct(incoming.sha...  31.6 us
    all_to_all x2, starting transfers between devices, exchange(): return lax.all_to_all(blocks, AXES, split_axis=0, concat_axis=0, tiled=True)  16.8 us
    unnamed x20, local copies, waits for them, and re-layouts  6.3 us
    pallas_call x1, Pallas kernels, total(): pl.pallas_call(total_kernel, out_shape=jax.ShapeDtypeStruct((owned, token...  4.62 us
  transfers between devices with their start and end apart: 2, of which 2 were waited for; matrix products, arithmetic and copies ran while one was open for 3% of the time, Pallas kernels for 0%

commit v1 on v0

v1 whole, which is shorter than its diff:
```python
import jax
import jax.numpy as jnp
from jax import lax
from jax.experimental import pallas as pl
from jax.experimental.pallas import tpu as pltpu
from jax.sharding import PartitionSpec as P

HEADS = 12
HD = 64
TOK = 16
AXES = ("img", "pair")
GROUP = 8
QUAD = 4
STEP = 32
BF16 = jnp.bfloat16
F32 = jnp.float32
MIB = 1024 * 1024
VMEM = pl.BlockSpec(memory_space=pltpu.VMEM)
SMEM = pl.BlockSpec(memory_space=pltpu.SMEM)
HBM = pl.BlockSpec(memory_space=pltpu.HBM)


def exchange(blocks):
    return lax.all_to_all(blocks, AXES, split_axis=0, concat_axis=0, tiled=True)


def dot(a, b, contract):
    return lax.dot_general(a, b, (contract, ((), ())), preferred_element_type=F32)


def normalised(values):
    mean = jnp.mean(values, axis=-1, keepdims=True)
    centred = values - mean
    spread = jnp.mean(centred * centred, axis=-1, keepdims=True)
    return centred * lax.rsqrt(spread + 1e-05)


def ask_kernel(owner_hbm, local_hbm, out, owner, local, sem):
    devices = out.shape[0]
    sides, slots = owner.shape
    copies = [
        pltpu.make_async_copy(owner_hbm, owner, sem.at[0]),
        pltpu.make_async_copy(local_hbm, local, sem.at[1]),
    ]
    for copy in copies:
        copy.start()
    for copy in copies:
        copy.wait()
    device = lax.broadcasted_iota(jnp.int32, (devices, slots), 0)
    found = jnp.zeros((devices, slots), jnp.int32)
    for side in range(sides):
        match = device == owner[side:side + 1, :]
        found = jnp.where(match, local[side:side + 1, :] + 1, found)
    wanted = jnp.sum(found, axis=1, keepdims=True) - 1
    out[...] = jnp.broadcast_to(wanted, out.shape)


def ask(owner, local, devices):
    return pl.pallas_call(
        ask_kernel,
        out_shape=jax.ShapeDtypeStruct((devices, devices), jnp.int32),
        in_specs=[HBM, HBM],
        out_specs=VMEM,
        scratch_shapes=[
            pltpu.VMEM(owner.shape, jnp.int32),
            pltpu.VMEM(owner.shape, jnp.int32),
            pltpu.SemaphoreType.DMA((2,)),
        ],
        compiler_params=pltpu.CompilerParams(vmem_limit_bytes=62 * MIB),
        name="ask",
    )(owner, local)


def fetch_kernel(rows, table, out, asked, scalars, sem, block_sem):
    devices = out.shape[0]
    owned = table.shape[0]
    square = rows.shape
    across = lax.broadcasted_iota(jnp.int32, square, 0) == lax.broadcasted_iota(jnp.int32, square, 1)
    asked[...] = jnp.sum(jnp.where(across, rows[...], 0), axis=0, keepdims=True)
    copy = pltpu.make_async_copy(asked, scalars, sem)
    copy.start()
    copy.wait()

    def send(d, carry):
        image = jnp.clip(scalars[0, d], 0, owned - 1)
        pltpu.make_async_copy(table.at[image], out.at[d], block_sem).start()
        return carry

    lax.fori_loop(0, devices, send, 0, unroll=8)
    pltpu.make_async_copy(out, out, block_sem).wait()


def fetch(rows, table):
    devices = rows.shape[0]
    return pl.pallas_call(
        fetch_kernel,
        out_shape=[
            jax.ShapeDtypeStruct((devices,) + table.shape[1:], table.dtype),
            jax.ShapeDtypeStruct((1, devices), jnp.int32),
        ],
        in_specs=[VMEM, VMEM],
        out_specs=[HBM, VMEM],
        scratch_shapes=[
            pltpu.SMEM((1, devices), jnp.int32),
            pltpu.SemaphoreType.DMA,
            pltpu.SemaphoreType.DMA,
        ],
        compiler_params=pltpu.CompilerParams(vmem_limit_bytes=61 * MIB),
        name="fetch",
    )(rows, table)


def decode_kernel(
    owner,
    incoming,
    gain_query,
    gain_key,
    gain_out,
    w_query_hbm,
    w_key_hbm,
    w_value_t_hbm,
    w_out_hbm,
    out,
    ends,
    result,
    attended_t,
    w_query,
    w_key,
    w_value_t,
    w_out,
    in_sem,
    weight_sem,
    out_sem,
):
    images, _, width = ends.shape
    rows = STEP * TOK
    block = GROUP * TOK

    loads = [
        pltpu.make_async_copy(w_query_hbm, w_query, weight_sem.at[0]),
        pltpu.make_async_copy(w_key_hbm, w_key, weight_sem.at[1]),
        pltpu.make_async_copy(w_value_t_hbm, w_value_t, weight_sem.at[2]),
        pltpu.make_async_copy(w_out_hbm, w_out, weight_sem.at[3]),
    ]

    def bring(it):
        for i in range(it * STEP, (it + 1) * STEP):
            device = owner[i % 2, i // 2]
            pltpu.make_async_copy(incoming.at[device], ends.at[i], in_sem.at[it]).start()

    bring(0)
    for load in loads:
        load.start()
    for it in range(1, images // STEP):
        bring(it)

    lane_image = lax.broadcasted_iota(jnp.int32, (TOK, block), 1) // TOK
    row_image = lax.broadcasted_iota(jnp.int32, (block, block), 0) // TOK
    column_image = lax.broadcasted_iota(jnp.int32, (block, block), 1) // TOK
    partner = ((row_image ^ 1) == column_image).astype(F32).astype(BF16)
    lane_head = lax.broadcasted_iota(jnp.int32, (block, QUAD * HD), 1) // HD
    head_mask = [(lane_head == h).astype(F32).astype(BF16) for h in range(QUAD)]
    to_query = gain_query[...].reshape(1, width)
    to_key = gain_key[...].reshape(1, width)
    to_out = gain_out[...].reshape(1, width)

    for it in range(images // STEP):
        here = ends.at[it * STEP:(it + 1) * STEP]
        pltpu.make_async_copy(here, here, in_sem.at[it]).wait()
        x = ends[it * STEP:(it + 1) * STEP].reshape(rows, width).astype(F32)
        xn = normalised(x)
        query_in = (xn * to_query).astype(BF16)
        context_in = (xn * to_key).astype(BF16)
        if it == 0:
            loads[0].wait()
        query = dot(query_in, w_query[...], ((1,), (0,))).astype(BF16)
        if it == 0:
            loads[1].wait()
        key = dot(context_in, w_key[...], ((1,), (0,))).astype(BF16)
        if it == 0:
            loads[2].wait()
        value_t = dot(w_value_t[...], context_in, ((1,), (1,))).astype(BF16)
        for g in range(rows // block):
            at = slice(g * block, (g + 1) * block)
            compact = []
            for c in range(HEADS // QUAD):
                lanes = slice(c * QUAD * HD, (c + 1) * QUAD * HD)
                masked = [key[at, lanes] * head_mask[h] for h in range(QUAD)]
                s_t = dot(jnp.concatenate(masked, axis=0), query[at, lanes], ((1,), (1,)))
                s_t = s_t.reshape(QUAD, GROUP, TOK, block)
                for h in range(QUAD):
                    scores = s_t[h, 1]
                    for i in range(1, GROUP):
                        scores = jnp.where(lane_image == i, s_t[h, i ^ 1], scores)
                    compact.append(scores)
            scores = jnp.stack(compact) * (HD ** -0.5)
            e = jnp.exp(scores - jnp.max(scores, axis=1, keepdims=True))
            weights = (e / jnp.sum(e, axis=1, keepdims=True)).astype(BF16)
            for head in range(HEADS):
                p_t = jnp.concatenate([weights[head]] * GROUP, axis=0) * partner
                features = slice(head * HD, (head + 1) * HD)
                attended_t[features, at] = dot(
                    value_t[features, at], p_t, ((1,), (0,))
                ).astype(BF16)
        if it == 0:
            loads[3].wait()
        hidden = x + dot(attended_t[...], w_out[...], ((0,), (0,)))
        head_in = (normalised(hidden) * to_out).astype(BF16)
        result[it * STEP:(it + 1) * STEP] = head_in.reshape(STEP, TOK, width)
        for i in range(it * STEP, (it + 1) * STEP):
            device = owner[i % 2, i // 2]
            pltpu.make_async_copy(result.at[i], out.at[device], out_sem).start()
    pltpu.make_async_copy(result, result, out_sem).wait()


def decode(owner, incoming, gain_query, gain_key, gain_out, w_query, w_key, w_value_t, w_out):
    images = owner.size
    devices, tokens, width = incoming.shape
    return pl.pallas_call(
        decode_kernel,
        out_shape=jax.ShapeDtypeStruct(incoming.shape, BF16),
        in_specs=[SMEM, HBM] + [VMEM] * 3 + [HBM] * 4,
        out_specs=HBM,
        scratch_shapes=[
            pltpu.VMEM((images, tokens, width), BF16),
            pltpu.VMEM((images, tokens, width), BF16),
            pltpu.VMEM((width, STEP * tokens), BF16),
            pltpu.VMEM(w_query.shape, BF16),
            pltpu.VMEM(w_key.shape, BF16),
            pltpu.VMEM(w_value_t.shape, BF16),
            pltpu.VMEM(w_out.shape, BF16),
            pltpu.SemaphoreType.DMA((images // STEP,)),
            pltpu.SemaphoreType.DMA((4,)),
            pltpu.SemaphoreType.DMA,
        ],
        compiler_params=pltpu.CompilerParams(vmem_limit_bytes=62 * MIB),
        name="decode",
    )(owner, incoming, gain_query, gain_key, gain_out, w_query, w_key, w_value_t, w_out)


def total_kernel(asked, returned, w_head, out, sums):
    devices, tokens, width = returned.shape
    owned = out.shape[0]
    sums[...] = jnp.zeros_like(sums)

    def add(d, carry):
        image = jnp.where(asked[0, d] >= 0, asked[0, d], owned)
        sums[image] += returned[d].astype(F32)
        return carry

    lax.fori_loop(0, devices, add, 0, unroll=4)
    whole = sums[:owned].reshape(owned * tokens, width)
    upper = whole.astype(BF16)
    lower = (whole - upper.astype(F32)).astype(BF16)
    head = dot(upper, w_head[...], ((1,), (0,))) + dot(lower, w_head[...], ((1,), (0,)))
    out[...] = head.astype(BF16).reshape(out.shape)


def total(asked, returned, w_head, owned):
    devices, tokens, width = returned.shape
    return pl.pallas_call(
        total_kernel,
        out_shape=jax.ShapeDtypeStruct((owned, tokens, w_head.shape[1]), BF16),
        in_specs=[SMEM, VMEM, VMEM],
        out_specs=VMEM,
        scratch_shapes=[pltpu.VMEM((owned + 1, tokens, width), F32)],
        compiler_params=pltpu.CompilerParams(vmem_limit_bytes=24 * MIB),
        name="total",
    )(asked, returned, w_head)


def on_device(
    encoder_tokens,
    pair_owner,
    pair_local,
    w_embed,
    gain_query,
    gain_key,
    gain_out,
    w_query,
    w_key,
    w_value,
    w_out,
    w_head,
):
    devices = lax.axis_size(AXES)
    owned, tokens, _ = encoder_tokens.shape
    owner = pair_owner.T
    rows = exchange(ask(owner, pair_local.T, devices))
    table = jnp.dot(
        encoder_tokens.reshape(owned * tokens, -1), w_embed, preferred_element_type=F32
    ).astype(BF16).reshape(owned, tokens, -1)
    outgoing, asked = fetch(rows, table)
    incoming = exchange(outgoing)
    going_back = decode(
        owner, incoming, gain_query, gain_key, gain_out, w_query, w_key, w_value.T, w_out
    )
    return total(asked, exchange(going_back), w_head, owned)


def solution(mesh):
    spec = P(AXES)
    return jax.shard_map(
        on_device,
        mesh=mesh,
        in_specs=(spec,) * 3 + (P(),) * 9,
        out_specs=spec,
        check_vma=False,
    )
```

time: 161 us -> 138 us (0.86)
  Pallas kernels: 39.1 us -> 24.7 us
  local copies, waits for them, and re-layouts: 7.34 us -> 2.07 us
  other arithmetic: 3.63 us -> 0 us
    pallas_call x1, Pallas kernels: 31.6 us -> 14.8 us  [decode(): pl.pallas_call(decode_kernel, out_shape=jax.ShapeDtypeStruct(incoming.sha...]
    unnamed x20 -> x11, local copies, waits for them, and re-layouts: 6.3 us -> 2.07 us
    all_to_all x1 -> x0, other arithmetic: 2.84 us -> none  [exchange(): return lax.all_to_all(blocks, AXES, split_axis=0, concat_axis=0, tiled=True)]
    pallas_call x1 -> x2, Pallas kernels: 2.83 us -> 5.49 us  [the longest x1 3.93 us: fetch(): pl.pallas_call(fetch_kernel, out_shape=[jax.ShapeDtypeStruct((devices,) +...]
where the time goes in v1:
time: 138 us
  waiting for transfers between devices  45.6 us (33%)
  blocking collectives  45.5 us (33%)
  Pallas kernels  24.7 us (18%)
  starting transfers between devices  16.8 us (12%)
  matrix products  3.09 us (2%)
  local copies, waits for them, and re-layouts  2.07 us (1%)
    all_to_all x2, waiting for transfers between devices, exchange(): return lax.all_to_all(blocks, AXES, split_axis=0, concat_axis=0, tiled=True)  45.6 us
    all_to_all x1, blocking collectives, exchange(): return lax.all_to_all(blocks, AXES, split_axis=0, concat_axis=0, tiled=True)  45.5 us
    all_to_all x2, starting transfers between devices, exchange(): return lax.all_to_all(blocks, AXES, split_axis=0, concat_axis=0, tiled=True)  16.8 us
    pallas_call x1, Pallas kernels, decode(): pl.pallas_call(decode_kernel, out_shape=jax.ShapeDtypeStruct(incoming.sha...  14.8 us
    pallas_call x1, Pallas kernels, total(): pl.pallas_call(total_kernel, out_shape=jax.ShapeDtypeStruct((owned, token...  4.39 us
    pallas_call x1, Pallas kernels, fetch(): pl.pallas_call(fetch_kernel, out_shape=[jax.ShapeDtypeStruct((devices,) +...  3.93 us
    dot_general x1, matrix products, on_device(): jnp.dot(encoder_tokens.reshape(owned * tokens, -1), w_embed, preferred_el...  3.09 us
  transfers between devices with their start and end apart: 2, of which 2 were waited for; matrix products, arithmetic and copies ran while one was open for 3% of the time, Pallas kernels for 0%

profile of v1, /device:TPU:1, one launch (start us, length us, event | category | flops | bytes accessed | tf_op | source)
XLA Modules:
  0.0 137.9 jit_solution(10424608410351181018)
XLA Ops:
  0.0 0.0 copy-start
  0.0 1.6 %ask.1 = s32[128,128]{1,0:T(8,128)} custom-call(s32[2,32]{1,0:T(2,128)} %bitcast.15, s32[2,32]{1,0:T(2,128)} %bitcast.17), custom_call_target="tpu_custom_call" | custom-call | tf_op jit(solution)/shard_map/ask/pallas_call | solution.py:59
  1.6 11.5 %all-to-all-start = ((s32[128,1,128]{2,1,0:T(1,128)}), s32[128,1,128]{2,1,0:T(1,128)S(1)}, u32[]{:S(2)}, u32[]{:S(2)}) async-start(s32[128,1,128]{2,1,0:T(1,128)} %bitcast.13), calls=%async_computation | async-start | bytes 131072 | tf_op jit(solution)/shard_map/all_to_all | solution.py:24
  13.1 0.0 copy-done
  13.1 3.1 %convolution_convert_fusion = bf16[512,768]{1,0:T(8,128)(2,1)} fusion(bf16[512,1024]{1,0:T(8,128)(2,1)} %bitcast.18, bf16[1024,768]{1,0:T(8,128)(2,1)S(1)} %copy-done), kind=kOutput, calls=%fused_computation | convolution fusion | flops 805699584 | bytes 3407872 | tf_op jit(solution)/shard_map/dot_general | solution.py:290
  16.2 6.7 %all-to-all-done = s32[128,1,128]{2,1,0:T(1,128)S(1)} async-done(((s32[128,1,128]{2,1,0:T(1,128)}), s32[128,1,128]{2,1,0:T(1,128)S(1)}, u32[]{:S(2)}, u32[]{:S(2)}) %all-to-all-start) | async-done | bytes 65568 | tf_op jit(solution)/shard_map/all_to_all | solution.py:24
  22.9 0.0 copy-start.4
  22.9 0.6 copy-done.4
  23.5 3.9 %fetch.1 = (bf16[128,16,768]{2,1,0:T(8,128)(2,1)}, s32[1,128]{1,0:T(1,128)}) custom-call(s32[128,128]{1,0:T(8,128)} %bitcast.14, bf16[32,16,768]{2,1,0:T(8,128)(2,1)} %bitcast.12), custom_call_target="tpu_custom_call" | custom-call | tf_op jit(solution)/shard_map/fetch/pallas_call | solution.py:95
  27.4 0.0 copy-start.3
  27.4 5.3 %all-to-all-start.1 = ((bf16[128,16,768]{2,1,0:T(8,128)(2,1)}), bf16[128,16,768]{2,1,0:T(8,128)(2,1)}, u32[]{:S(2)}, u32[]{:S(2)}) async-start(bf16[128,16,768]{2,1,0:T(8,128)(2,1)} %get-tuple-element.8), calls=%async_computation.1 | async-start | bytes 6291456 | tf_op jit(solution)/shard_map/all_to_all | solution.py:24
  32.7 0.0 copy-done.3
  32.8 1.4 %copy.15 = bf16[768,768]{0,1:T(8,128)(2,1)} copy(bf16[768,768]{1,0:T(8,128)(2,1)S(1)} %copy-done.3) | data formatting | bytes 2359296 | tf_op args[9]
  34.2 38.9 %all-to-all-done.1.incoming = bf16[128,16,768]{2,1,0:T(8,128)(2,1)} async-done(((bf16[128,16,768]{2,1,0:T(8,128)(2,1)}), bf16[128,16,768]{2,1,0:T(8,128)(2,1)}, u32[]{:S(2)}, u32[]{:S(2)}) %all-to-all-start.1) | async-done | bytes 3145760 | tf_op jit(solution)/shard_map/all_to_all | solution.py:24
  73.1 14.8 %decode.1 = bf16[128,16,768]{2,1,0:T(8,128)(2,1)} custom-call(s32[2,32]{1,0:T(2,128)} %bitcast.16, bf16[128,16,768]{2,1,0:T(8,128)(2,1)} %all-to-all-done.1.incoming, f32[768]{0:T(1024)} %gain_query.1, f32[768]{0:T(1024)} %gain_key.1, f32[768]{0:T(1024)} %gain_out.1, bf16[768,768]{1,0:T(8,128)(2,1)} %w_query_hbm.1, bf16[768,768]{1,0:T(8,128)(2,1)} %w_key_hbm.1, ...), custom_call_target="tpu_custom_call" | custom-call | tf_op jit(solution)/shard_map/decode/pallas_call | solution.py:219
  88.0 0.0 copy-start.1
  88.0 0.0 copy-start.2
  88.0 45.5 %all_to_all.21.returned = bf16[128,16,768]{2,1,0:T(8,128)(2,1)S(1)} all-to-all(bf16[128,16,768]{2,1,0:T(8,128)(2,1)} %decode.1), channel_id=1, replica_groups=mesh['img'=8,'pair'=16] {'img','pair'}, dimensions={0} | all-to-all | bytes 6291456 | tf_op jit(solution)/shard_map/all_to_all | solution.py:24
  133.5 0.0 copy-done.1
  133.5 0.0 copy-done.2
  133.5 4.4 %total.1 = bf16[32,16,1024]{2,1,0:T(8,128)(2,1)} custom-call(s32[1,128]{1,0:T(1,128)S(1)} %copy-done.2, bf16[128,16,768]{2,1,0:T(8,128)(2,1)S(1)} %all_to_all.21.returned, bf16[768,1024]{1,0:T(8,128)(2,1)S(1)} %copy-done.1), custom_call_target="tpu_custom_call" | custom-call | tf_op jit(solution)/shard_map/total/pallas_call | solution.py:261
Async XLA Ops:
  0.0 13.1 %copy-start = (bf16[1024,768]{1,0:T(8,128)(2,1)S(1)}, bf16[1024,768]{1,0:T(8,128)(2,1)}, u32[]{:S(2)}) copy-start(bf16[1024,768]{1,0:T(8,128)(2,1)} %param.15) | copy-start | bytes 4718596
  1.6 21.3 %all-to-all-start = ((s32[128,1,128]{2,1,0:T(1,128)}), s32[128,1,128]{2,1,0:T(1,128)S(1)}, u32[]{:S(2)}, u32[]{:S(2)}) async-start(s32[128,1,128]{2,1,0:T(1,128)} %bitcast.13), calls=%async_computation | async-start | bytes 131072 | tf_op jit(solution)/shard_map/all_to_all | solution.py:24
  22.9 0.6 copy-start.4
  27.4 5.3 %copy-start.3 = (bf16[768,768]{1,0:T(8,128)(2,1)S(1)}, bf16[768,768]{1,0:T(8,128)(2,1)}, u32[]{:S(2)}) copy-start(bf16[768,768]{1,0:T(8,128)(2,1)} %param.21) | copy-start | bytes 3538948
  27.4 45.7 %all-to-all-start.1 = ((bf16[128,16,768]{2,1,0:T(8,128)(2,1)}), bf16[128,16,768]{2,1,0:T(8,128)(2,1)}, u32[]{:S(2)}, u32[]{:S(2)}) async-start(bf16[128,16,768]{2,1,0:T(8,128)(2,1)} %get-tuple-element.8), calls=%async_computation.1 | async-start | bytes 6291456 | tf_op jit(solution)/shard_map/all_to_all | solution.py:24
  88.0 45.5 %copy-start.1 = (bf16[768,1024]{1,0:T(8,128)(2,1)S(1)}, bf16[768,1024]{1,0:T(8,128)(2,1)}, u32[]{:S(2)}) copy-start(bf16[768,1024]{1,0:T(8,128)(2,1)} %w_head.1) | copy-start | bytes 4718596
  88.0 45.5 %copy-start.2 = (s32[1,128]{1,0:T(1,128)S(1)}, s32[1,128]{1,0:T(1,128)}, u32[]{:S(2)}) copy-start(s32[1,128]{1,0:T(1,128)} %get-tuple-element.7.asked) | copy-start | bytes 1540

commit v2 on v1

v2 whole, which is shorter than its diff:
```python
import jax
import jax.numpy as jnp
from jax import lax
from jax.experimental import pallas as pl
from jax.experimental.pallas import tpu as pltpu
from jax.sharding import PartitionSpec as P

HEADS = 12
HD = 64
TOK = 16
AXES = ("img", "pair")
GROUP = 8
QUAD = 4
STEP = 32
BF16 = jnp.bfloat16
F32 = jnp.float32
MIB = 1024 * 1024
VMEM = pl.BlockSpec(memory_space=pltpu.VMEM)
SMEM = pl.BlockSpec(memory_space=pltpu.SMEM)
HBM = pl.BlockSpec(memory_space=pltpu.HBM)


def exchange(blocks):
    return lax.all_to_all(blocks, AXES, split_axis=0, concat_axis=0, tiled=True)


def dot(a, b, contract):
    return lax.dot_general(a, b, (contract, ((), ())), preferred_element_type=F32)


def normalised(values):
    mean = jnp.mean(values, axis=-1, keepdims=True)
    centred = values - mean
    spread = jnp.mean(centred * centred, axis=-1, keepdims=True)
    return centred * lax.rsqrt(spread + 1e-05)


def ask_kernel(owner_hbm, local_hbm, out, owner, local, sem):
    devices = out.shape[0]
    sides, slots = owner.shape
    copies = [
        pltpu.make_async_copy(owner_hbm, owner, sem.at[0]),
        pltpu.make_async_copy(local_hbm, local, sem.at[1]),
    ]
    for copy in copies:
        copy.start()
    for copy in copies:
        copy.wait()
    device = lax.broadcasted_iota(jnp.int32, (devices, slots), 0)
    found = jnp.zeros((devices, slots), jnp.int32)
    for side in range(sides):
        match = device == owner[side:side + 1, :]
        found = jnp.where(match, local[side:side + 1, :] + 1, found)
    wanted = jnp.sum(found, axis=1, keepdims=True) - 1
    out[...] = jnp.broadcast_to(wanted, out.shape)


def ask(owner, local, devices):
    return pl.pallas_call(
        ask_kernel,
        out_shape=jax.ShapeDtypeStruct((devices, devices), jnp.int32),
        in_specs=[HBM, HBM],
        out_specs=VMEM,
        scratch_shapes=[
            pltpu.VMEM(owner.shape, jnp.int32),
            pltpu.VMEM(owner.shape, jnp.int32),
            pltpu.SemaphoreType.DMA((2,)),
        ],
        compiler_params=pltpu.CompilerParams(vmem_limit_bytes=62 * MIB),
        name="ask",
    )(owner, local)


def fetch_kernel(rows, table, out, asked, scalars, sem):
    devices = out.shape[0]
    owned = table.shape[0]
    square = rows.shape
    across = lax.broadcasted_iota(jnp.int32, square, 0) == lax.broadcasted_iota(jnp.int32, square, 1)
    asked[...] = jnp.sum(jnp.where(across, rows[...], 0), axis=0, keepdims=True)
    copy = pltpu.make_async_copy(asked, scalars, sem)
    copy.start()
    copy.wait()
    for d in range(devices):
        out[d] = table[jnp.clip(scalars[0, d], 0, owned - 1)]


def fetch(rows, table):
    devices = rows.shape[0]
    return pl.pallas_call(
        fetch_kernel,
        out_shape=[
            jax.ShapeDtypeStruct((devices,) + table.shape[1:], table.dtype),
            jax.ShapeDtypeStruct((1, devices), jnp.int32),
        ],
        in_specs=[VMEM, VMEM],
        out_specs=[VMEM, VMEM],
        scratch_shapes=[pltpu.SMEM((1, devices), jnp.int32), pltpu.SemaphoreType.DMA],
        compiler_params=pltpu.CompilerParams(vmem_limit_bytes=16 * MIB),
        name="fetch",
    )(rows, table)


def decode_kernel(
    owner,
    incoming,
    gain_query,
    gain_key,
    gain_out,
    w_query,
    w_key,
    w_value,
    w_out,
    out,
    attended_t,
    w_value_t,
):
    images = owner.shape[0] * owner.shape[1]
    width = incoming.shape[2]
    rows = STEP * TOK
    block = GROUP * TOK

    lane_image = lax.broadcasted_iota(jnp.int32, (TOK, block), 1) // TOK
    row_image = lax.broadcasted_iota(jnp.int32, (block, block), 0) // TOK
    column_image = lax.broadcasted_iota(jnp.int32, (block, block), 1) // TOK
    partner = ((row_image ^ 1) == column_image).astype(F32).astype(BF16)
    lane_head = lax.broadcasted_iota(jnp.int32, (block, QUAD * HD), 1) // HD
    head_mask = [(lane_head == h).astype(F32).astype(BF16) for h in range(QUAD)]
    to_query = gain_query[...].reshape(1, width)
    to_key = gain_key[...].reshape(1, width)
    to_out = gain_out[...].reshape(1, width)

    for it in range(images // STEP):
        here = [owner[i % 2, i // 2] for i in range(it * STEP, (it + 1) * STEP)]
        x = jnp.stack([incoming[device] for device in here]).reshape(rows, width).astype(F32)
        xn = normalised(x)
        query_in = (xn * to_query).astype(BF16)
        context_in = (xn * to_key).astype(BF16)
        query = dot(query_in, w_query[...], ((1,), (0,))).astype(BF16)
        key = dot(context_in, w_key[...], ((1,), (0,))).astype(BF16)
        if it == 0:
            w_value_t[...] = w_value[...].T
        value_t = dot(w_value_t[...], context_in, ((1,), (1,))).astype(BF16)

        def score(g):
            at = slice(g * block, (g + 1) * block)
            compact = []
            for c in range(HEADS // QUAD):
                lanes = slice(c * QUAD * HD, (c + 1) * QUAD * HD)
                masked = [key[at, lanes] * head_mask[h] for h in range(QUAD)]
                s_t = dot(jnp.concatenate(masked, axis=0), query[at, lanes], ((1,), (1,)))
                s_t = s_t.reshape(QUAD, GROUP, TOK, block)
                for h in range(QUAD):
                    scores = s_t[h, 1]
                    for i in range(1, GROUP):
                        scores = jnp.where(lane_image == i, s_t[h, i ^ 1], scores)
                    compact.append(scores)
            return jnp.stack(compact) * (HD ** -0.5)

        def softmax(scores):
            e = jnp.exp(scores - jnp.max(scores, axis=1, keepdims=True))
            return (e / jnp.sum(e, axis=1, keepdims=True)).astype(BF16)

        def attend(g, weights):
            at = slice(g * block, (g + 1) * block)
            for head in range(HEADS):
                p_t = jnp.concatenate([weights[head]] * GROUP, axis=0) * partner
                features = slice(head * HD, (head + 1) * HD)
                attended_t[features, at] = dot(
                    value_t[features, at], p_t, ((1,), (0,))
                ).astype(BF16)

        groups = rows // block
        scores, weights = score(0), None
        for g in range(groups + 1):
            later = score(g + 1) if g + 1 < groups else None
            if weights is not None:
                attend(g - 1, weights)
            weights = softmax(scores) if scores is not None else None
            scores = later
        hidden = x + dot(attended_t[...], w_out[...], ((0,), (0,)))
        head_in = (normalised(hidden) * to_out).astype(BF16).reshape(STEP, TOK, width)
        for i in range(STEP):
            out[here[i]] = head_in[i]


def decode(owner, incoming, *parameters):
    images = owner.size
    devices, tokens, width = incoming.shape
    return pl.pallas_call(
        decode_kernel,
        out_shape=jax.ShapeDtypeStruct(incoming.shape, BF16),
        in_specs=[SMEM] + [VMEM] * 8,
        out_specs=VMEM,
        scratch_shapes=[
            pltpu.VMEM((width, STEP * tokens), BF16),
            pltpu.VMEM((width, width), BF16),
        ],
        compiler_params=pltpu.CompilerParams(vmem_limit_bytes=40 * MIB),
        name="decode",
    )(owner, incoming, *parameters)


def total_kernel(asked, returned, w_head, out, even, odd, result, sem):
    devices, tokens, width = returned.shape
    owned = out.shape[0]
    even[...] = jnp.zeros_like(even)
    odd[...] = jnp.zeros_like(odd)
    for d in range(devices):
        sums = odd if d % 2 else even
        image = jnp.where(asked[0, d] >= 0, asked[0, d], owned)
        sums[image] += returned[d].astype(F32)
    part = owned // sem.shape[0]
    copies = []
    for n in range(sem.shape[0]):
        at = slice(n * part, (n + 1) * part)
        whole = (even[at] + odd[at]).reshape(part * tokens, width).astype(BF16)
        head = dot(whole, w_head[...], ((1,), (0,))).astype(BF16)
        result[at] = head.reshape(part, tokens, w_head.shape[1])
        copies.append(pltpu.make_async_copy(result.at[at], out.at[at], sem.at[n]))
        copies[-1].start()
    for copy in copies:
        copy.wait()


def total(asked, returned, w_head, owned):
    devices, tokens, width = returned.shape
    shape = (owned, tokens, w_head.shape[1])
    return pl.pallas_call(
        total_kernel,
        out_shape=jax.ShapeDtypeStruct(shape, BF16),
        in_specs=[SMEM, VMEM, VMEM],
        out_specs=HBM,
        scratch_shapes=[
            pltpu.VMEM((owned + 1, tokens, width), F32),
            pltpu.VMEM((owned + 1, tokens, width), F32),
            pltpu.VMEM(shape, BF16),
            pltpu.SemaphoreType.DMA((2,)),
        ],
        compiler_params=pltpu.CompilerParams(vmem_limit_bytes=24 * MIB),
        name="total",
    )(asked, returned, w_head)


def on_device(
    encoder_tokens,
    pair_owner,
    pair_local,
    w_embed,
    gain_query,
    gain_key,
    gain_out,
    w_query,
    w_key,
    w_value,
    w_out,
    w_head,
):
    devices = lax.axis_size(AXES)
    owned, tokens, _ = encoder_tokens.shape
    owner = pair_owner.T
    rows = exchange(ask(owner, pair_local.T, devices))
    table = jnp.dot(
        encoder_tokens.reshape(owned * tokens, -1), w_embed, preferred_element_type=F32
    ).astype(BF16).reshape(owned, tokens, -1)
    outgoing, asked = fetch(rows, table)
    incoming = exchange(outgoing)
    going_back = decode(
        owner, incoming, gain_query, gain_key, gain_out, w_query, w_key, w_value, w_out
    )
    return total(asked, exchange(going_back), w_head, owned)


def solution(mesh):
    spec = P(AXES)
    return jax.shard_map(
        on_device,
        mesh=mesh,
        in_specs=(spec,) * 3 + (P(),) * 9,
        out_specs=spec,
        check_vma=False,
    )
```

time: 138 us -> 127 us (0.920)
  blocking collectives: 45.5 us -> 89.9 us
  waiting for transfers between devices: 45.6 us -> 7.49 us
  Pallas kernels: 24.7 us -> 15.1 us
  starting transfers between devices: 16.8 us -> 11.5 us
  local copies, waits for them, and re-layouts: 2.07 us -> 0.06 us
    all_to_all x1 -> x2, blocking collectives: 45.5 us -> 89.9 us  [exchange(): return lax.all_to_all(blocks, AXES, split_axis=0, concat_axis=0, tiled=True)]
    all_to_all x2 -> x1, waiting for transfers between devices: 45.6 us -> 7.49 us  [exchange(): return lax.all_to_all(blocks, AXES, split_axis=0, concat_axis=0, tiled=True)]
    all_to_all x2 -> x1, starting transfers between devices: 16.8 us -> 11.5 us  [exchange(): return lax.all_to_all(blocks, AXES, split_axis=0, concat_axis=0, tiled=True)]
    pallas_call x1, Pallas kernels: 14.8 us -> 9.6 us  [decode(): pl.pallas_call(decode_kernel, out_shape=jax.ShapeDtypeStruct(incoming.sha...]
    pallas_call x1, Pallas kernels: 3.93 us -> 0.83 us  [fetch(): pl.pallas_call(fetch_kernel, out_shape=[jax.ShapeDtypeStruct((devices,) +...]
    unnamed x11 -> x20, local copies, waits for them, and re-layouts: 2.07 us -> 0.06 us
  transfers between devices with their start and end apart: 2 -> 1, of which waited for: 2 -> 1; matrix products, arithmetic and copies ran while one was open for 3% -> 2% of each run, Pallas kernels for 0% -> 0%
where the time goes in v2:
time: 127 us; the launch traced here: 126 us
  blocking collectives  89.9 us (71%)
  Pallas kernels  15.1 us (12%)
  starting transfers between devices  11.5 us (9%)
  waiting for transfers between devices  7.49 us (6%)
  matrix products  2.2 us (2%)
    all_to_all x2, blocking collectives, exchange(): return lax.all_to_all(blocks, AXES, split_axis=0, concat_axis=0, tiled=True)  89.9 us
    all_to_all x1, starting transfers between devices, exchange(): return lax.all_to_all(blocks, AXES, split_axis=0, concat_axis=0, tiled=True)  11.5 us
    pallas_call x1, Pallas kernels, decode(): pl.pallas_call(decode_kernel, out_shape=jax.ShapeDtypeStruct(incoming.sha...  9.6 us
    all_to_all x1, waiting for transfers between devices, exchange(): return lax.all_to_all(blocks, AXES, split_axis=0, concat_axis=0, tiled=True)  7.49 us
    pallas_call x1, Pallas kernels, total(): pl.pallas_call(total_kernel, out_shape=jax.ShapeDtypeStruct(shape, BF16),...  3.06 us
  transfers between devices with their start and end apart: 1, of which 1 were waited for; matrix products, arithmetic and copies ran while one was open for 2% of the time, Pallas kernels for 0%

profile of v2, /device:TPU:1, one launch (start us, length us, event | category | flops | bytes accessed | tf_op | source)
XLA Modules:
  0.0 126.3 jit_solution(464635885162604992)
XLA Ops:
  0.0 0.0 copy-start
  0.0 1.6 %ask.1 = s32[128,128]{1,0:T(8,128)} custom-call(s32[2,32]{1,0:T(2,128)} %bitcast.12, s32[2,32]{1,0:T(2,128)} %bitcast.15), custom_call_target="tpu_custom_call" | custom-call | tf_op jit(solution)/shard_map/ask/pallas_call | solution.py:59
  1.6 11.5 %all-to-all-start = ((s32[128,1,128]{2,1,0:T(1,128)}), s32[128,1,128]{2,1,0:T(1,128)S(1)}, u32[]{:S(2)}, u32[]{:S(2)}) async-start(s32[128,1,128]{2,1,0:T(1,128)} %bitcast.14), calls=%async_computation | async-start | bytes 131072 | tf_op jit(solution)/shard_map/all_to_all | solution.py:24
  13.1 0.0 copy-done
  13.1 2.2 %convolution_convert_fusion = bf16[512,768]{1,0:T(8,128)(2,1)S(1)} fusion(bf16[512,1024]{1,0:T(8,128)(2,1)} %bitcast.16, bf16[1024,768]{1,0:T(8,128)(2,1)S(1)} %copy-done), kind=kOutput, calls=%fused_computation | convolution fusion | flops 805699584 | bytes 3407872 | tf_op jit(solution)/shard_map/dot_general | solution.py:262
  15.3 7.5 %all-to-all-done = s32[128,1,128]{2,1,0:T(1,128)S(1)} async-done(((s32[128,1,128]{2,1,0:T(1,128)}), s32[128,1,128]{2,1,0:T(1,128)S(1)}, u32[]{:S(2)}, u32[]{:S(2)}) %all-to-all-start) | async-done | bytes 65568 | tf_op jit(solution)/shard_map/all_to_all | solution.py:24
  22.8 0.8 fetch.1
  23.6 0.0 copy-start.2
  23.7 0.0 copy-start.3
  23.7 0.0 copy-start.4
  23.7 0.0 copy-start.5
  23.7 0.0 copy-start.6
  23.7 0.0 copy-start.7
  23.7 0.0 copy-start.8
  23.7 0.0 copy-start.9
  23.7 44.6 %all_to_all.21.incoming = bf16[128,16,768]{2,1,0:T(8,128)(2,1)S(1)} all-to-all(bf16[128,16,768]{2,1,0:T(8,128)(2,1)S(1)} %get-tuple-element.8), channel_id=1, replica_groups=mesh['img'=8,'pair'=16] {'img','pair'}, dimensions={0} | all-to-all | bytes 6291456 | tf_op jit(solution)/shard_map/all_to_all | solution.py:24
  68.4 0.0 copy-done.2
  68.4 0.0 copy-done.3
  68.4 0.0 copy-done.4
  68.4 0.0 copy-done.5
  68.4 0.0 copy-done.6
  68.4 0.0 copy-done.7
  68.4 0.0 copy-done.8
  68.4 0.0 copy-done.9
  68.4 9.6 %decode.1 = bf16[128,16,768]{2,1,0:T(8,128)(2,1)S(1)} custom-call(s32[2,32]{1,0:T(2,128)S(1)} %bitcast.13, bf16[128,16,768]{2,1,0:T(8,128)(2,1)S(1)} %all_to_all.21.incoming, f32[768]{0:T(1024)S(1)} %copy-done.6, f32[768]{0:T(1024)S(1)} %copy-done.7, f32[768]{0:T(1024)S(1)} %copy-done.8, bf16[768,768]{1,0:T(8,128)(2,1)S(1)} %copy-done.2, ...), custom_call_target="tpu_custom_call" | custom-call | tf_op jit(solution)/shard_map/decode/pallas_call | solution.py:189
  78.0 0.0 copy-start.1
  78.0 45.2 %all_to_all.22.returned = bf16[128,16,768]{2,1,0:T(8,128)(2,1)S(1)} all-to-all(bf16[128,16,768]{2,1,0:T(8,128)(2,1)S(1)} %decode.1), channel_id=1, replica_groups=mesh['img'=8,'pair'=16] {'img','pair'}, dimensions={0} | all-to-all | bytes 6291456 | tf_op jit(solution)/shard_map/all_to_all | solution.py:24
  123.3 0.0 copy-done.1
  123.3 3.1 %total.1 = bf16[32,16,1024]{2,1,0:T(8,128)(2,1)} custom-call(s32[1,128]{1,0:T(1,128)S(1)} %get-tuple-element.7.asked, bf16[128,16,768]{2,1,0:T(8,128)(2,1)S(1)} %all_to_all.22.returned, bf16[768,1024]{1,0:T(8,128)(2,1)S(1)} %copy-done.1), custom_call_target="tpu_custom_call" | custom-call | tf_op jit(solution)/shard_map/total/pallas_call | solution.py:228
Async XLA Ops:
  0.0 13.1 %copy-start = (bf16[1024,768]{1,0:T(8,128)(2,1)S(1)}, bf16[1024,768]{1,0:T(8,128)(2,1)}, u32[]{:S(2)}) copy-start(bf16[1024,768]{1,0:T(8,128)(2,1)} %param.15) | copy-start | bytes 4718596
  1.6 21.2 %all-to-all-start = ((s32[128,1,128]{2,1,0:T(1,128)}), s32[128,1,128]{2,1,0:T(1,128)S(1)}, u32[]{:S(2)}, u32[]{:S(2)}) async-start(s32[128,1,128]{2,1,0:T(1,128)} %bitcast.14), calls=%async_computation | async-start | bytes 131072 | tf_op jit(solution)/shard_map/all_to_all | solution.py:24
  23.6 44.7 %copy-start.2 = (bf16[768,768]{1,0:T(8,128)(2,1)S(1)}, bf16[768,768]{1,0:T(8,128)(2,1)}, u32[]{:S(2)}) copy-start(bf16[768,768]{1,0:T(8,128)(2,1)} %w_query.1) | copy-start | bytes 3538948
  23.7 44.7 %copy-start.3 = (bf16[768,768]{1,0:T(8,128)(2,1)S(1)}, bf16[768,768]{1,0:T(8,128)(2,1)}, u32[]{:S(2)}) copy-start(bf16[768,768]{1,0:T(8,128)(2,1)} %w_key.1) | copy-start | bytes 3538948
  23.7 44.7 %copy-start.4 = (bf16[768,768]{1,0:T(8,128)(2,1)S(1)}, bf16[768,768]{1,0:T(8,128)(2,1)}, u32[]{:S(2)}) copy-start(bf16[768,768]{1,0:T(8,128)(2,1)} %w_value.1) | copy-start | bytes 3538948
  23.7 44.7 %copy-start.5 = (bf16[768,768]{1,0:T(8,128)(2,1)S(1)}, bf16[768,768]{1,0:T(8,128)(2,1)}, u32[]{:S(2)}) copy-start(bf16[768,768]{1,0:T(8,128)(2,1)} %w_out.1) | copy-start | bytes 3538948
  23.7 44.7 %copy-start.6 = (f32[768]{0:T(1024)S(1)}, f32[768]{0:T(1024)}, u32[]{:S(2)}) copy-start(f32[768]{0:T(1024)} %gain_query.1) | copy-start | bytes 9220
  23.7 44.7 %copy-start.7 = (f32[768]{0:T(1024)S(1)}, f32[768]{0:T(1024)}, u32[]{:S(2)}) copy-start(f32[768]{0:T(1024)} %gain_key.1) | copy-start | bytes 9220
  23.7 44.7 %copy-start.8 = (f32[768]{0:T(1024)S(1)}, f32[768]{0:T(1024)}, u32[]{:S(2)}) copy-start(f32[768]{0:T(1024)} %gain_out.1) | copy-start | bytes 9220
  23.7 44.7 %copy-start.9 = (s32[32,2]{0,1:T(2,128)S(1)}, s32[32,2]{0,1:T(2,128)}, u32[]{:S(2)}) copy-start(s32[32,2]{0,1:T(2,128)} %param.13) | copy-start | bytes 772
  78.0 45.2 %copy-start.1 = (bf16[768,1024]{1,0:T(8,128)(2,1)S(1)}, bf16[768,1024]{1,0:T(8,128)(2,1)}, u32[]{:S(2)}) copy-start(bf16[768,1024]{1,0:T(8,128)(2,1)} %w_head.1) | copy-start | bytes 4718596

commit v3 on v2

--- a/solution.py
+++ b/solution.py
@@ -123,8 +123,10 @@
     row_image = lax.broadcasted_iota(jnp.int32, (block, block), 0) // TOK
     column_image = lax.broadcasted_iota(jnp.int32, (block, block), 1) // TOK
     partner = ((row_image ^ 1) == column_image).astype(F32).astype(BF16)
+    partner = jnp.concatenate([partner, partner], axis=1)
     lane_head = lax.broadcasted_iota(jnp.int32, (block, QUAD * HD), 1) // HD
-    head_mask = [(lane_head == h).astype(F32).astype(BF16) for h in range(QUAD)]
+    low_mask = [(lane_head % 2 == n).astype(F32).astype(BF16) for n in range(2)]
+    high_mask = [(lane_head // 2 == n).astype(F32).astype(BF16) for n in range(2)]
     to_query = gain_query[...].reshape(1, width)
     to_key = gain_key[...].reshape(1, width)
     to_out = gain_out[...].reshape(1, width)
@@ -146,13 +148,16 @@
             compact = []
             for c in range(HEADS // QUAD):
                 lanes = slice(c * QUAD * HD, (c + 1) * QUAD * HD)
-                masked = [key[at, lanes] * head_mask[h] for h in range(QUAD)]
-                s_t = dot(jnp.concatenate(masked, axis=0), query[at, lanes], ((1,), (1,)))
-                s_t = s_t.reshape(QUAD, GROUP, TOK, block)
+                keys = [key[at, lanes] * low_mask[n] for n in range(2)]
+                queries = [query[at, lanes] * high_mask[n] for n in range(2)]
+                s_t = dot(
+                    jnp.concatenate(keys, axis=0), jnp.concatenate(queries, axis=0), ((1,), (1,))
+                ).reshape(2, GROUP, TOK, 2 * block)
                 for h in range(QUAD):
-                    scores = s_t[h, 1]
+                    part = slice(h // 2 * block, (h // 2 + 1) * block)
+                    scores = s_t[h % 2, 1, :, part]
                     for i in range(1, GROUP):
-                        scores = jnp.where(lane_image == i, s_t[h, i ^ 1], scores)
+                        scores = jnp.where(lane_image == i, s_t[h % 2, i ^ 1, :, part], scores)
                     compact.append(scores)
             return jnp.stack(compact) * (HD ** -0.5)
 
@@ -162,12 +167,13 @@
 
         def attend(g, weights):
             at = slice(g * block, (g + 1) * block)
-            for head in range(HEADS):
-                p_t = jnp.concatenate([weights[head]] * GROUP, axis=0) * partner
-                features = slice(head * HD, (head + 1) * HD)
-                attended_t[features, at] = dot(
-                    value_t[features, at], p_t, ((1,), (0,))
-                ).astype(BF16)
+            for head in range(0, HEADS, 2):
+                two = jnp.concatenate([weights[head], weights[head + 1]], axis=1)
+                p_t = jnp.concatenate([two] * GROUP, axis=0) * partner
+                features = slice(head * HD, (head + 2) * HD)
+                both = dot(value_t[features, at], p_t, ((1,), (0,))).astype(BF16)
+                attended_t[head * HD:(head + 1) * HD, at] = both[:HD, :block]
+                attended_t[(head + 1) * HD:(head + 2) * HD, at] = both[HD:, block:]
 
         groups = rows // block
         scores, weights = score(0), None

time: 127 us -> 126 us (level)
  no operation moved by 1% of the time
where the time goes in v3:
time: 126 us
  blocking collectives  89.9 us (71%)
  Pallas kernels  14.3 us (11%)
  starting transfers between devices  11.5 us (9%)
  waiting for transfers between devices  7.49 us (6%)
  matrix products  2.2 us (2%)
    all_to_all x2, blocking collectives, exchange(): return lax.all_to_all(blocks, AXES, split_axis=0, concat_axis=0, tiled=True)  89.9 us
    all_to_all x1, starting transfers between devices, exchange(): return lax.all_to_all(blocks, AXES, split_axis=0, concat_axis=0, tiled=True)  11.5 us
    pallas_call x1, Pallas kernels, decode(): pl.pallas_call(decode_kernel, out_shape=jax.ShapeDtypeStruct(incoming.sha...  8.79 us
    all_to_all x1, waiting for transfers between devices, exchange(): return lax.all_to_all(blocks, AXES, split_axis=0, concat_axis=0, tiled=True)  7.49 us
    pallas_call x1, Pallas kernels, total(): pl.pallas_call(total_kernel, out_shape=jax.ShapeDtypeStruct(shape, BF16),...  3.06 us
  transfers between devices with their start and end apart: 1, of which 1 were waited for; matrix products, arithmetic and copies ran while one was open for 2% of the time, Pallas kernels for 0%

profile of v3, /device:TPU:1, one launch (start us, length us, event | category | flops | bytes accessed | tf_op | source)
XLA Modules:
  0.0 125.5 jit_solution(13050415344416024974)
XLA Ops:
  0.0 0.0 copy-start
  0.0 1.6 %ask.1 = s32[128,128]{1,0:T(8,128)} custom-call(s32[2,32]{1,0:T(2,128)} %bitcast.12, s32[2,32]{1,0:T(2,128)} %bitcast.15), custom_call_target="tpu_custom_call" | custom-call | tf_op jit(solution)/shard_map/ask/pallas_call | solution.py:59
  1.6 11.5 %all-to-all-start = ((s32[128,1,128]{2,1,0:T(1,128)}), s32[128,1,128]{2,1,0:T(1,128)S(1)}, u32[]{:S(2)}, u32[]{:S(2)}) async-start(s32[128,1,128]{2,1,0:T(1,128)} %bitcast.14), calls=%async_computation | async-start | bytes 131072 | tf_op jit(solution)/shard_map/all_to_all | solution.py:24
  13.1 0.0 copy-done
  13.1 2.2 %convolution_convert_fusion = bf16[512,768]{1,0:T(8,128)(2,1)S(1)} fusion(bf16[512,1024]{1,0:T(8,128)(2,1)} %bitcast.16, bf16[1024,768]{1,0:T(8,128)(2,1)S(1)} %copy-done), kind=kOutput, calls=%fused_computation | convolution fusion | flops 805699584 | bytes 3407872 | tf_op jit(solution)/shard_map/dot_general | solution.py:268
  15.3 7.5 %all-to-all-done = s32[128,1,128]{2,1,0:T(1,128)S(1)} async-done(((s32[128,1,128]{2,1,0:T(1,128)}), s32[128,1,128]{2,1,0:T(1,128)S(1)}, u32[]{:S(2)}, u32[]{:S(2)}) %all-to-all-start) | async-done | bytes 65568 | tf_op jit(solution)/shard_map/all_to_all | solution.py:24
  22.8 0.8 fetch.1
  23.6 0.0 copy-start.2
  23.7 0.0 copy-start.3
  23.7 0.0 copy-start.4
  23.7 0.0 copy-start.5
  23.7 0.0 copy-start.6
  23.7 0.0 copy-start.7
  23.7 0.0 copy-start.8
  23.7 0.0 copy-start.9
  23.7 44.6 %all_to_all.21.incoming = bf16[128,16,768]{2,1,0:T(8,128)(2,1)S(1)} all-to-all(bf16[128,16,768]{2,1,0:T(8,128)(2,1)S(1)} %get-tuple-element.8), channel_id=1, replica_groups=mesh['img'=8,'pair'=16] {'img','pair'}, dimensions={0} | all-to-all | bytes 6291456 | tf_op jit(solution)/shard_map/all_to_all | solution.py:24
  68.4 0.0 copy-done.2
  68.4 0.0 copy-done.3
  68.4 0.0 copy-done.4
  68.4 0.0 copy-done.5
  68.4 0.0 copy-done.6
  68.4 0.0 copy-done.7
  68.4 0.0 copy-done.8
  68.4 0.0 copy-done.9
  68.4 8.8 %decode.1 = bf16[128,16,768]{2,1,0:T(8,128)(2,1)S(1)} custom-call(s32[2,32]{1,0:T(2,128)S(1)} %bitcast.13, bf16[128,16,768]{2,1,0:T(8,128)(2,1)S(1)} %all_to_all.21.incoming, f32[768]{0:T(1024)S(1)} %copy-done.6, f32[768]{0:T(1024)S(1)} %copy-done.7, f32[768]{0:T(1024)S(1)} %copy-done.8, bf16[768,768]{1,0:T(8,128)(2,1)S(1)} %copy-done.2, ...), custom_call_target="tpu_custom_call" | custom-call | tf_op jit(solution)/shard_map/decode/pallas_call | solution.py:195
  77.2 0.0 copy-start.1
  77.2 45.2 %all_to_all.22.returned = bf16[128,16,768]{2,1,0:T(8,128)(2,1)S(1)} all-to-all(bf16[128,16,768]{2,1,0:T(8,128)(2,1)S(1)} %decode.1), channel_id=1, replica_groups=mesh['img'=8,'pair'=16] {'img','pair'}, dimensions={0} | all-to-all | bytes 6291456 | tf_op jit(solution)/shard_map/all_to_all | solution.py:24
  122.5 0.0 copy-done.1
  122.5 3.1 %total.1 = bf16[32,16,1024]{2,1,0:T(8,128)(2,1)} custom-call(s32[1,128]{1,0:T(1,128)S(1)} %get-tuple-element.7.asked, bf16[128,16,768]{2,1,0:T(8,128)(2,1)S(1)} %all_to_all.22.returned, bf16[768,1024]{1,0:T(8,128)(2,1)S(1)} %copy-done.1), custom_call_target="tpu_custom_call" | custom-call | tf_op jit(solution)/shard_map/total/pallas_call | solution.py:234
Async XLA Ops:
  0.0 13.1 %copy-start = (bf16[1024,768]{1,0:T(8,128)(2,1)S(1)}, bf16[1024,768]{1,0:T(8,128)(2,1)}, u32[]{:S(2)}) copy-start(bf16[1024,768]{1,0:T(8,128)(2,1)} %param.15) | copy-start | bytes 4718596
  1.6 21.2 %all-to-all-start = ((s32[128,1,128]{2,1,0:T(1,128)}), s32[128,1,128]{2,1,0:T(1,128)S(1)}, u32[]{:S(2)}, u32[]{:S(2)}) async-start(s32[128,1,128]{2,1,0:T(1,128)} %bitcast.14), calls=%async_computation | async-start | bytes 131072 | tf_op jit(solution)/shard_map/all_to_all | solution.py:24
  23.6 44.7 %copy-start.2 = (bf16[768,768]{1,0:T(8,128)(2,1)S(1)}, bf16[768,768]{1,0:T(8,128)(2,1)}, u32[]{:S(2)}) copy-start(bf16[768,768]{1,0:T(8,128)(2,1)} %w_query.1) | copy-start | bytes 3538948
  23.7 44.7 %copy-start.3 = (bf16[768,768]{1,0:T(8,128)(2,1)S(1)}, bf16[768,768]{1,0:T(8,128)(2,1)}, u32[]{:S(2)}) copy-start(bf16[768,768]{1,0:T(8,128)(2,1)} %w_key.1) | copy-start | bytes 3538948
  23.7 44.7 %copy-start.4 = (bf16[768,768]{1,0:T(8,128)(2,1)S(1)}, bf16[768,768]{1,0:T(8,128)(2,1)}, u32[]{:S(2)}) copy-start(bf16[768,768]{1,0:T(8,128)(2,1)} %w_value.1) | copy-start | bytes 3538948
  23.7 44.7 %copy-start.5 = (bf16[768,768]{1,0:T(8,128)(2,1)S(1)}, bf16[768,768]{1,0:T(8,128)(2,1)}, u32[]{:S(2)}) copy-start(bf16[768,768]{1,0:T(8,128)(2,1)} %w_out.1) | copy-start | bytes 3538948
  23.7 44.7 %copy-start.6 = (f32[768]{0:T(1024)S(1)}, f32[768]{0:T(1024)}, u32[]{:S(2)}) copy-start(f32[768]{0:T(1024)} %gain_query.1) | copy-start | bytes 9220
  23.7 44.7 %copy-start.7 = (f32[768]{0:T(1024)S(1)}, f32[768]{0:T(1024)}, u32[]{:S(2)}) copy-start(f32[768]{0:T(1024)} %gain_key.1) | copy-start | bytes 9220
  23.7 44.7 %copy-start.8 = (f32[768]{0:T(1024)S(1)}, f32[768]{0:T(1024)}, u32[]{:S(2)}) copy-start(f32[768]{0:T(1024)} %gain_out.1) | copy-start | bytes 9220
  23.7 44.7 %copy-start.9 = (s32[32,2]{0,1:T(2,128)S(1)}, s32[32,2]{0,1:T(2,128)}, u32[]{:S(2)}) copy-start(s32[32,2]{0,1:T(2,128)} %param.13) | copy-start | bytes 772
  77.2 45.2 %copy-start.1 = (bf16[768,1024]{1,0:T(8,128)(2,1)S(1)}, bf16[768,1024]{1,0:T(8,128)(2,1)}, u32[]{:S(2)}) copy-start(bf16[768,1024]{1,0:T(8,128)(2,1)} %w_head.1) | copy-start | bytes 4718596

commit v4 on v3

--- a/solution.py
+++ b/solution.py
@@ -183,7 +183,13 @@
                 attend(g - 1, weights)
             weights = softmax(scores) if scores is not None else None
             scores = later
-        hidden = x + dot(attended_t[...], w_out[...], ((0,), (0,)))
+        hidden = jnp.concatenate(
+            [
+                x[n:n + 2 * block] + dot(attended_t[:, n:n + 2 * block], w_out[...], ((0,), (0,)))
+                for n in range(0, rows, 2 * block)
+            ],
+            axis=0,
+        )
         head_in = (normalised(hidden) * to_out).astype(BF16).reshape(STEP, TOK, width)
         for i in range(STEP):
             out[here[i]] = head_in[i]
@@ -206,19 +212,23 @@
     )(owner, incoming, *parameters)
 
 
-def total_kernel(asked, returned, w_head, out, even, odd, result, sem):
+def total_kernel(asked_vmem, returned, w_head, out, even, odd, result, asked, sem, asked_sem):
     devices, tokens, width = returned.shape
     owned = out.shape[0]
+    copy = pltpu.make_async_copy(asked_vmem, asked, asked_sem)
+    copy.start()
     even[...] = jnp.zeros_like(even)
     odd[...] = jnp.zeros_like(odd)
+    copy.wait()
     for d in range(devices):
         sums = odd if d % 2 else even
         image = jnp.where(asked[0, d] >= 0, asked[0, d], owned)
         sums[image] += returned[d].astype(F32)
-    part = owned // sem.shape[0]
     copies = []
+    cuts = (0, owned // 2, 3 * owned // 4, owned)
     for n in range(sem.shape[0]):
-        at = slice(n * part, (n + 1) * part)
+        at = slice(cuts[n], cuts[n + 1])
+        part = cuts[n + 1] - cuts[n]
         whole = (even[at] + odd[at]).reshape(part * tokens, width).astype(BF16)
         head = dot(whole, w_head[...], ((1,), (0,))).astype(BF16)
         result[at] = head.reshape(part, tokens, w_head.shape[1])
@@ -234,13 +244,15 @@
     return pl.pallas_call(
         total_kernel,
         out_shape=jax.ShapeDtypeStruct(shape, BF16),
-        in_specs=[SMEM, VMEM, VMEM],
+        in_specs=[VMEM, VMEM, VMEM],
         out_specs=HBM,
         scratch_shapes=[
             pltpu.VMEM((owned + 1, tokens, width), F32),
             pltpu.VMEM((owned + 1, tokens, width), F32),
             pltpu.VMEM(shape, BF16),
-            pltpu.SemaphoreType.DMA((2,)),
+            pltpu.SMEM(asked.shape, jnp.int32),
+            pltpu.SemaphoreType.DMA((3,)),
+            pltpu.SemaphoreType.DMA,
         ],
         compiler_params=pltpu.CompilerParams(vmem_limit_bytes=24 * MIB),
         name="total",

time: 126 us -> 125 us (level)
  no operation moved by 1% of the time
where the time goes in v4:
time: 125 us
  blocking collectives  89.9 us (72%)
  Pallas kernels  13.5 us (11%)
  starting transfers between devices  11.5 us (9%)
  waiting for transfers between devices  7.49 us (6%)
  matrix products  2.2 us (2%)
    all_to_all x2, blocking collectives, exchange(): return lax.all_to_all(blocks, AXES, split_axis=0, concat_axis=0, tiled=True)  89.9 us
    all_to_all x1, starting transfers between devices, exchange(): return lax.all_to_all(blocks, AXES, split_axis=0, concat_axis=0, tiled=True)  11.5 us
    pallas_call x1, Pallas kernels, decode(): pl.pallas_call(decode_kernel, out_shape=jax.ShapeDtypeStruct(incoming.sha...  8.31 us
    all_to_all x1, waiting for transfers between devices, exchange(): return lax.all_to_all(blocks, AXES, split_axis=0, concat_axis=0, tiled=True)  7.49 us
    pallas_call x1, Pallas kernels, total(): pl.pallas_call(total_kernel, out_shape=jax.ShapeDtypeStruct(shape, BF16),...  2.8 us
  transfers between devices with their start and end apart: 1, of which 1 were waited for; matrix products, arithmetic and copies ran while one was open for 2% of the time, Pallas kernels for 0%

profile of v4, /device:TPU:1, one launch (start us, length us, event | category | flops | bytes accessed | tf_op | source)
XLA Modules:
  0.0 124.8 jit_solution(12638937933604890925)
XLA Ops:
  0.0 0.0 copy-start
  0.0 1.6 %ask.1 = s32[128,128]{1,0:T(8,128)} custom-call(s32[2,32]{1,0:T(2,128)} %bitcast.12, s32[2,32]{1,0:T(2,128)} %bitcast.15), custom_call_target="tpu_custom_call" | custom-call | tf_op jit(solution)/shard_map/ask/pallas_call | solution.py:59
  1.6 11.5 %all-to-all-start = ((s32[128,1,128]{2,1,0:T(1,128)}), s32[128,1,128]{2,1,0:T(1,128)S(1)}, u32[]{:S(2)}, u32[]{:S(2)}) async-start(s32[128,1,128]{2,1,0:T(1,128)} %bitcast.14), calls=%async_computation | async-start | bytes 131072 | tf_op jit(solution)/shard_map/all_to_all | solution.py:24
  13.1 0.0 copy-done
  13.1 2.2 %convolution_convert_fusion = bf16[512,768]{1,0:T(8,128)(2,1)S(1)} fusion(bf16[512,1024]{1,0:T(8,128)(2,1)} %bitcast.16, bf16[1024,768]{1,0:T(8,128)(2,1)S(1)} %copy-done), kind=kOutput, calls=%fused_computation | convolution fusion | flops 805699584 | bytes 3407872 | tf_op jit(solution)/shard_map/dot_general | solution.py:280
  15.3 7.5 %all-to-all-done = s32[128,1,128]{2,1,0:T(1,128)S(1)} async-done(((s32[128,1,128]{2,1,0:T(1,128)}), s32[128,1,128]{2,1,0:T(1,128)S(1)}, u32[]{:S(2)}, u32[]{:S(2)}) %all-to-all-start) | async-done | bytes 65568 | tf_op jit(solution)/shard_map/all_to_all | solution.py:24
  22.8 0.8 fetch.1
  23.6 0.0 copy-start.2
  23.7 0.0 copy-start.3
  23.7 0.0 copy-start.4
  23.7 0.0 copy-start.5
  23.7 0.0 copy-start.6
  23.7 0.0 copy-start.7
  23.7 0.0 copy-start.8
  23.7 0.0 copy-start.9
  23.7 44.6 %all_to_all.21.incoming = bf16[128,16,768]{2,1,0:T(8,128)(2,1)S(1)} all-to-all(bf16[128,16,768]{2,1,0:T(8,128)(2,1)S(1)} %get-tuple-element.8), channel_id=1, replica_groups=mesh['img'=8,'pair'=16] {'img','pair'}, dimensions={0} | all-to-all | bytes 6291456 | tf_op jit(solution)/shard_map/all_to_all | solution.py:24
  68.4 0.0 copy-done.2
  68.4 0.0 copy-done.3
  68.4 0.0 copy-done.4
  68.4 0.0 copy-done.5
  68.4 0.0 copy-done.6
  68.4 0.0 copy-done.7
  68.4 0.0 copy-done.8
  68.4 0.0 copy-done.9
  68.4 8.3 %decode.1 = bf16[128,16,768]{2,1,0:T(8,128)(2,1)S(1)} custom-call(s32[2,32]{1,0:T(2,128)S(1)} %bitcast.13, bf16[128,16,768]{2,1,0:T(8,128)(2,1)S(1)} %all_to_all.21.incoming, f32[768]{0:T(1024)S(1)} %copy-done.6, f32[768]{0:T(1024)S(1)} %copy-done.7, f32[768]{0:T(1024)S(1)} %copy-done.8, bf16[768,768]{1,0:T(8,128)(2,1)S(1)} %copy-done.2, ...), custom_call_target="tpu_custom_call" | custom-call | tf_op jit(solution)/shard_map/decode/pallas_call | solution.py:201
  76.7 0.0 copy-start.1
  76.8 45.2 %all_to_all.22.returned = bf16[128,16,768]{2,1,0:T(8,128)(2,1)S(1)} all-to-all(bf16[128,16,768]{2,1,0:T(8,128)(2,1)S(1)} %decode.1), channel_id=1, replica_groups=mesh['img'=8,'pair'=16] {'img','pair'}, dimensions={0} | all-to-all | bytes 6291456 | tf_op jit(solution)/shard_map/all_to_all | solution.py:24
  122.0 0.0 copy-done.1
  122.0 2.8 %total.1 = bf16[32,16,1024]{2,1,0:T(8,128)(2,1)} custom-call(s32[1,128]{1,0:T(1,128)S(1)} %get-tuple-element.7.asked_vmem, bf16[128,16,768]{2,1,0:T(8,128)(2,1)S(1)} %all_to_all.22.returned, bf16[768,1024]{1,0:T(8,128)(2,1)S(1)} %copy-done.1), custom_call_target="tpu_custom_call" | custom-call | tf_op jit(solution)/shard_map/total/pallas_call | solution.py:244
Async XLA Ops:
  0.0 13.1 %copy-start = (bf16[1024,768]{1,0:T(8,128)(2,1)S(1)}, bf16[1024,768]{1,0:T(8,128)(2,1)}, u32[]{:S(2)}) copy-start(bf16[1024,768]{1,0:T(8,128)(2,1)} %param.15) | copy-start | bytes 4718596
  1.6 21.2 %all-to-all-start = ((s32[128,1,128]{2,1,0:T(1,128)}), s32[128,1,128]{2,1,0:T(1,128)S(1)}, u32[]{:S(2)}, u32[]{:S(2)}) async-start(s32[128,1,128]{2,1,0:T(1,128)} %bitcast.14), calls=%async_computation | async-start | bytes 131072 | tf_op jit(solution)/shard_map/all_to_all | solution.py:24
  23.6 44.7 %copy-start.2 = (bf16[768,768]{1,0:T(8,128)(2,1)S(1)}, bf16[768,768]{1,0:T(8,128)(2,1)}, u32[]{:S(2)}) copy-start(bf16[768,768]{1,0:T(8,128)(2,1)} %w_query.1) | copy-start | bytes 3538948
  23.7 44.7 %copy-start.3 = (bf16[768,768]{1,0:T(8,128)(2,1)S(1)}, bf16[768,768]{1,0:T(8,128)(2,1)}, u32[]{:S(2)}) copy-start(bf16[768,768]{1,0:T(8,128)(2,1)} %w_key.1) | copy-start | bytes 3538948
  23.7 44.7 %copy-start.4 = (bf16[768,768]{1,0:T(8,128)(2,1)S(1)}, bf16[768,768]{1,0:T(8,128)(2,1)}, u32[]{:S(2)}) copy-start(bf16[768,768]{1,0:T(8,128)(2,1)} %w_value.1) | copy-start | bytes 3538948
  23.7 44.7 %copy-start.5 = (bf16[768,768]{1,0:T(8,128)(2,1)S(1)}, bf16[768,768]{1,0:T(8,128)(2,1)}, u32[]{:S(2)}) copy-start(bf16[768,768]{1,0:T(8,128)(2,1)} %w_out.1) | copy-start | bytes 3538948
  23.7 44.7 %copy-start.6 = (f32[768]{0:T(1024)S(1)}, f32[768]{0:T(1024)}, u32[]{:S(2)}) copy-start(f32[768]{0:T(1024)} %gain_query.1) | copy-start | bytes 9220
  23.7 44.7 %copy-start.7 = (f32[768]{0:T(1024)S(1)}, f32[768]{0:T(1024)}, u32[]{:S(2)}) copy-start(f32[768]{0:T(1024)} %gain_key.1) | copy-start | bytes 9220
  23.7 44.7 %copy-start.8 = (f32[768]{0:T(1024)S(1)}, f32[768]{0:T(1024)}, u32[]{:S(2)}) copy-start(f32[768]{0:T(1024)} %gain_out.1) | copy-start | bytes 9220
  23.7 44.7 %copy-start.9 = (s32[32,2]{0,1:T(2,128)S(1)}, s32[32,2]{0,1:T(2,128)}, u32[]{:S(2)}) copy-start(s32[32,2]{0,1:T(2,128)} %param.13) | copy-start | bytes 772
  76.7 45.2 %copy-start.1 = (bf16[768,1024]{1,0:T(8,128)(2,1)S(1)}, bf16[768,1024]{1,0:T(8,128)(2,1)}, u32[]{:S(2)}) copy-start(bf16[768,1024]{1,0:T(8,128)(2,1)} %w_head.1) | copy-start | bytes 4718596

commit v5 on v4

--- a/solution.py
+++ b/solution.py
@@ -137,8 +137,11 @@
         xn = normalised(x)
         query_in = (xn * to_query).astype(BF16)
         context_in = (xn * to_key).astype(BF16)
-        query = dot(query_in, w_query[...], ((1,), (0,))).astype(BF16)
-        key = dot(context_in, w_key[...], ((1,), (0,))).astype(BF16)
+        pieces = [slice(n, n + 2 * block) for n in range(0, rows, 2 * block)]
+        query, key = (
+            jnp.concatenate([dot(a[n], w[...], ((1,), (0,))).astype(BF16) for n in pieces], axis=0)
+            for a, w in ((query_in, w_query), (context_in, w_key))
+        )
         if it == 0:
             w_value_t[...] = w_value[...].T
         value_t = dot(w_value_t[...], context_in, ((1,), (1,))).astype(BF16)

time: 125 us -> 125 us (level)
  no operation moved by 1% of the time
where the time goes in v5:
time: 125 us
  blocking collectives  89.8 us (72%)
  Pallas kernels  13.5 us (11%)
  starting transfers between devices  11.5 us (9%)
  waiting for transfers between devices  7.49 us (6%)
  matrix products  2.2 us (2%)
    all_to_all x2, blocking collectives, exchange(): return lax.all_to_all(blocks, AXES, split_axis=0, concat_axis=0, tiled=True)  89.8 us
    all_to_all x1, starting transfers between devices, exchange(): return lax.all_to_all(blocks, AXES, split_axis=0, concat_axis=0, tiled=True)  11.5 us
    pallas_call x1, Pallas kernels, decode(): pl.pallas_call(decode_kernel, out_shape=jax.ShapeDtypeStruct(incoming.sha...  8.27 us
    all_to_all x1, waiting for transfers between devices, exchange(): return lax.all_to_all(blocks, AXES, split_axis=0, concat_axis=0, tiled=True)  7.49 us
    pallas_call x1, Pallas kernels, total(): pl.pallas_call(total_kernel, out_shape=jax.ShapeDtypeStruct(shape, BF16),...  2.8 us
  transfers between devices with their start and end apart: 1, of which 1 were waited for; matrix products, arithmetic and copies ran while one was open for 2% of the time, Pallas kernels for 0%

profile of v5, /device:TPU:1, one launch (start us, length us, event | category | flops | bytes accessed | tf_op | source)
XLA Modules:
  0.0 124.7 jit_solution(3241372784179897326)
XLA Ops:
  0.0 0.0 copy-start
  0.0 1.6 %ask.1 = s32[128,128]{1,0:T(8,128)} custom-call(s32[2,32]{1,0:T(2,128)} %bitcast.12, s32[2,32]{1,0:T(2,128)} %bitcast.15), custom_call_target="tpu_custom_call" | custom-call | tf_op jit(solution)/shard_map/ask/pallas_call | solution.py:59
  1.6 11.5 %all-to-all-start = ((s32[128,1,128]{2,1,0:T(1,128)}), s32[128,1,128]{2,1,0:T(1,128)S(1)}, u32[]{:S(2)}, u32[]{:S(2)}) async-start(s32[128,1,128]{2,1,0:T(1,128)} %bitcast.14), calls=%async_computation | async-start | bytes 131072 | tf_op jit(solution)/shard_map/all_to_all | solution.py:24
  13.1 0.0 copy-done
  13.1 2.2 %convolution_convert_fusion = bf16[512,768]{1,0:T(8,128)(2,1)S(1)} fusion(bf16[512,1024]{1,0:T(8,128)(2,1)} %bitcast.16, bf16[1024,768]{1,0:T(8,128)(2,1)S(1)} %copy-done), kind=kOutput, calls=%fused_computation | convolution fusion | flops 805699584 | bytes 3407872 | tf_op jit(solution)/shard_map/dot_general | solution.py:283
  15.3 7.5 %all-to-all-done = s32[128,1,128]{2,1,0:T(1,128)S(1)} async-done(((s32[128,1,128]{2,1,0:T(1,128)}), s32[128,1,128]{2,1,0:T(1,128)S(1)}, u32[]{:S(2)}, u32[]{:S(2)}) %all-to-all-start) | async-done | bytes 65568 | tf_op jit(solution)/shard_map/all_to_all | solution.py:24
  22.8 0.8 fetch.1
  23.6 0.0 copy-start.2
  23.7 0.0 copy-start.3
  23.7 0.0 copy-start.4
  23.7 0.0 copy-start.5
  23.7 0.0 copy-start.6
  23.7 0.0 copy-start.7
  23.7 0.0 copy-start.8
  23.7 0.0 copy-start.9
  23.7 44.6 %all_to_all.21.incoming = bf16[128,16,768]{2,1,0:T(8,128)(2,1)S(1)} all-to-all(bf16[128,16,768]{2,1,0:T(8,128)(2,1)S(1)} %get-tuple-element.8), channel_id=1, replica_groups=mesh['img'=8,'pair'=16] {'img','pair'}, dimensions={0} | all-to-all | bytes 6291456 | tf_op jit(solution)/shard_map/all_to_all | solution.py:24
  68.4 0.0 copy-done.2
  68.4 0.0 copy-done.3
  68.4 0.0 copy-done.4
  68.4 0.0 copy-done.5
  68.4 0.0 copy-done.6
  68.4 0.0 copy-done.7
  68.4 0.0 copy-done.8
  68.4 0.0 copy-done.9
  68.4 8.3 %decode.1 = bf16[128,16,768]{2,1,0:T(8,128)(2,1)S(1)} custom-call(s32[2,32]{1,0:T(2,128)S(1)} %bitcast.13, bf16[128,16,768]{2,1,0:T(8,128)(2,1)S(1)} %all_to_all.21.incoming, f32[768]{0:T(1024)S(1)} %copy-done.6, f32[768]{0:T(1024)S(1)} %copy-done.7, f32[768]{0:T(1024)S(1)} %copy-done.8, bf16[768,768]{1,0:T(8,128)(2,1)S(1)} %copy-done.2, ...), custom_call_target="tpu_custom_call" | custom-call | tf_op jit(solution)/shard_map/decode/pallas_call | solution.py:204
  76.7 0.0 copy-start.1
  76.7 45.2 %all_to_all.22.returned = bf16[128,16,768]{2,1,0:T(8,128)(2,1)S(1)} all-to-all(bf16[128,16,768]{2,1,0:T(8,128)(2,1)S(1)} %decode.1), channel_id=1, replica_groups=mesh['img'=8,'pair'=16] {'img','pair'}, dimensions={0} | all-to-all | bytes 6291456 | tf_op jit(solution)/shard_map/all_to_all | solution.py:24
  121.9 0.0 copy-done.1
  121.9 2.8 %total.1 = bf16[32,16,1024]{2,1,0:T(8,128)(2,1)} custom-call(s32[1,128]{1,0:T(1,128)S(1)} %get-tuple-element.7.asked_vmem, bf16[128,16,768]{2,1,0:T(8,128)(2,1)S(1)} %all_to_all.22.returned, bf16[768,1024]{1,0:T(8,128)(2,1)S(1)} %copy-done.1), custom_call_target="tpu_custom_call" | custom-call | tf_op jit(solution)/shard_map/total/pallas_call | solution.py:247
Async XLA Ops:
  0.0 13.1 %copy-start = (bf16[1024,768]{1,0:T(8,128)(2,1)S(1)}, bf16[1024,768]{1,0:T(8,128)(2,1)}, u32[]{:S(2)}) copy-start(bf16[1024,768]{1,0:T(8,128)(2,1)} %param.15) | copy-start | bytes 4718596
  1.6 21.2 %all-to-all-start = ((s32[128,1,128]{2,1,0:T(1,128)}), s32[128,1,128]{2,1,0:T(1,128)S(1)}, u32[]{:S(2)}, u32[]{:S(2)}) async-start(s32[128,1,128]{2,1,0:T(1,128)} %bitcast.14), calls=%async_computation | async-start | bytes 131072 | tf_op jit(solution)/shard_map/all_to_all | solution.py:24
  23.6 44.7 %copy-start.2 = (bf16[768,768]{1,0:T(8,128)(2,1)S(1)}, bf16[768,768]{1,0:T(8,128)(2,1)}, u32[]{:S(2)}) copy-start(bf16[768,768]{1,0:T(8,128)(2,1)} %w_query.1) | copy-start | bytes 3538948
  23.7 44.7 %copy-start.3 = (bf16[768,768]{1,0:T(8,128)(2,1)S(1)}, bf16[768,768]{1,0:T(8,128)(2,1)}, u32[]{:S(2)}) copy-start(bf16[768,768]{1,0:T(8,128)(2,1)} %w_key.1) | copy-start | bytes 3538948
  23.7 44.7 %copy-start.4 = (bf16[768,768]{1,0:T(8,128)(2,1)S(1)}, bf16[768,768]{1,0:T(8,128)(2,1)}, u32[]{:S(2)}) copy-start(bf16[768,768]{1,0:T(8,128)(2,1)} %w_value.1) | copy-start | bytes 3538948
  23.7 44.7 %copy-start.5 = (bf16[768,768]{1,0:T(8,128)(2,1)S(1)}, bf16[768,768]{1,0:T(8,128)(2,1)}, u32[]{:S(2)}) copy-start(bf16[768,768]{1,0:T(8,128)(2,1)} %w_out.1) | copy-start | bytes 3538948
  23.7 44.7 %copy-start.6 = (f32[768]{0:T(1024)S(1)}, f32[768]{0:T(1024)}, u32[]{:S(2)}) copy-start(f32[768]{0:T(1024)} %gain_query.1) | copy-start | bytes 9220
  23.7 44.7 %copy-start.7 = (f32[768]{0:T(1024)S(1)}, f32[768]{0:T(1024)}, u32[]{:S(2)}) copy-start(f32[768]{0:T(1024)} %gain_key.1) | copy-start | bytes 9220
  23.7 44.7 %copy-start.8 = (f32[768]{0:T(1024)S(1)}, f32[768]{0:T(1024)}, u32[]{:S(2)}) copy-start(f32[768]{0:T(1024)} %gain_out.1) | copy-start | bytes 9220
  23.7 44.7 %copy-start.9 = (s32[32,2]{0,1:T(2,128)S(1)}, s32[32,2]{0,1:T(2,128)}, u32[]{:S(2)}) copy-start(s32[32,2]{0,1:T(2,128)} %param.13) | copy-start | bytes 772
  76.7 45.2 %copy-start.1 = (bf16[768,1024]{1,0:T(8,128)(2,1)S(1)}, bf16[768,1024]{1,0:T(8,128)(2,1)}, u32[]{:S(2)}) copy-start(bf16[768,1024]{1,0:T(8,128)(2,1)} %w_head.1) | copy-start | bytes 4718596
